TPU v7x, 32 devices: a whole 2x2x4 slice. The times are simulated.
32 devices in a mesh: batch: 4 (over x, core), seq: 8 (over z, y).
Axes of the slice: x: 2, y: 2, z: 4, core: 2. Of those that a mesh axis runs over, the one named last changes fastest.
Arguments:
- tokens: bfloat16 [32, 2048, 768], P('batch', 'seq'), may hold values from -6 to 6
- segment_ids: int32 [32, 2048], P('batch', 'seq'), may hold values from -1 to 7, as said below
- query_weight: bfloat16 [768, 768], replicated, may hold values from -0.21875 to 0.21875
- query_bias: float32 [768], replicated, may hold values from -1.75 to 1.75
- keyval_weight: bfloat16 [768, 128], replicated, may hold values from -0.21875 to 0.21875
- keyval_bias: float32 [128], replicated, may hold values from -1.75 to 1.75
- out_weight: bfloat16 [768, 768], replicated, may hold values from -1.25 to 1.25
- out_bias: float32 [768], replicated, may hold values from -1.75 to 1.75
- up_weight: bfloat16 [768, 3072], replicated, may hold values from -0.21875 to 0.21875
- up_bias: float32 [3072], replicated, may hold values from -1.75 to 1.75
- down_weight: bfloat16 [3072, 768], replicated, may hold values from -0.109375 to 0.109375
- down_bias: float32 [768], replicated, may hold values from -1.75 to 1.75
- attention_gain: float32 [768], replicated, may hold values from 0.5 to 1.5
- attention_shift: float32 [768], replicated, may hold values from -1.75 to 1.75
- dense_gain: float32 [768], replicated, may hold values from 0.5 to 1.5
- dense_shift: float32 [768], replicated, may hold values from -1.75 to 1.75
- out_cotangent: bfloat16 [32, 2048, 768], P('batch', 'seq'), may hold values from -6 to 6
- keyval_cotangent: bfloat16 [32, 2048, 128], P('batch', 'seq'), may hold values from -1.75 to 1.75
Outputs:
- layer_out: bfloat16 [32, 2048, 768], P('batch', 'seq')
- keyval_out: bfloat16 [32, 2048, 128], P('batch', 'seq')
- grad_tokens: bfloat16 [32, 2048, 768], P('batch', 'seq')
- grad_query_weight: float32 [768, 768], P('seq')
- grad_query_bias: float32 [768], P('seq')
- grad_keyval_weight: float32 [768, 128], P('seq')
- grad_keyval_bias: float32 [128], P('seq')
- grad_out_weight: float32 [768, 768], P('seq')
- grad_out_bias: float32 [768], P('seq')
- grad_up_weight: float32 [768, 3072], P('seq')
- grad_up_bias: float32 [3072], P('seq')
- grad_down_weight: float32 [3072, 768], P('seq')
- grad_down_bias: float32 [768], P('seq')
- grad_attention_gain: float32 [768], P('seq')
- grad_attention_shift: float32 [768], P('seq')
- grad_dense_gain: float32 [768], P('seq')
- grad_dense_shift: float32 [768], P('seq')
Inputs may be any that keep to these rules, and one draw needn't show every extreme that they name: `segment_ids`: within a row the ids of documents start at 0 and never fall, each step up by one, and every document has one position or more; in each group of 8 consecutive rows one row, drawn from the seed, is a single document 0 over all 2048 positions with no padding; each of the other 7 rows of the group holds eight documents with ids 0 to 7 followed by a nonempty tail of padding -1.
All inputs are finite; a program needn't handle non-finite values.
Results may differ from a plain program's by a relative error of at most 0.018.
Values may be sent and summed in bfloat16 or wider, within the bound.
A program may use at most 256 MiB of HBM per device.

v0:
```python
from functools import partial

import jax
import jax.numpy as jnp
from jax import lax
from jax.sharding import PartitionSpec as P

HEADS = 12
HEAD_DIM = 64
ROT = 16


epsilon = 1e-05
rope_base = 10000.0
negative = -1e30


def layer_norm(values, gain_vector, shift_vector):
    average = jnp.mean(values, axis=-1, keepdims=True)
    centred = values - average
    variance = jnp.mean(centred * centred, axis=-1, keepdims=True)
    return centred * lax.rsqrt(variance + epsilon) * gain_vector + shift_vector


def rotary_tables(positions):
    half_rot = ROT // 2
    frequency = rope_base ** (-(2.0 * jnp.arange(half_rot, dtype=jnp.float32)) / ROT)
    angles = positions.astype(jnp.float32)[:, None] * frequency[None, :]
    return (jnp.cos(angles), jnp.sin(angles))


def rotate(values, cos_table, sin_table):
    half_rot = ROT // 2
    first_half = values[..., :half_rot]
    second_half = values[..., half_rot:ROT]
    return jnp.concatenate(
        [
            first_half * cos_table - second_half * sin_table,
            second_half * cos_table + first_half * sin_table,
            values[..., ROT:],
        ],
        axis=-1,
    )


def unrotate(values, cos_table, sin_table):
    half_rot = ROT // 2
    first_half = values[..., :half_rot]
    second_half = values[..., half_rot:ROT]
    return jnp.concatenate(
        [
            first_half * cos_table + second_half * sin_table,
            second_half * cos_table - first_half * sin_table,
            values[..., ROT:],
        ],
        axis=-1,
    )


def contract_rows(left_side, right_side):
    return lax.dot_general(
        left_side, right_side, (((0,), (0,)), ((), ())), preferred_element_type=jnp.float32
    )


def contract_cols(left_side, right_side):
    return lax.dot_general(
        left_side, right_side, (((1,), (1,)), ((), ())), preferred_element_type=jnp.float32
    )


def local(
    tokens,
    segment_ids,
    query_weight,
    query_bias,
    keyval_weight,
    keyval_bias,
    out_weight,
    out_bias,
    up_weight,
    up_bias,
    down_weight,
    down_bias,
    attention_gain,
    attention_shift,
    dense_gain,
    dense_shift,
    out_cotangent,
    keyval_cotangent,
):
    rows, local_len, width = tokens.shape
    full_len = local_len * lax.axis_size("seq")
    tok_count = rows * local_len
    offset = lax.axis_index("seq") * local_len
    positions = offset + jnp.arange(local_len, dtype=jnp.int32)
    key_positions = jnp.arange(full_len, dtype=jnp.int32)
    score_scale = HEAD_DIM ** (-0.5)
    inputs = tokens.astype(jnp.float32).reshape(tok_count, width)
    valid_rows = (segment_ids >= 0).astype(jnp.float32).reshape(tok_count, 1)
    normed_full, attention_pull = jax.vjp(layer_norm, inputs, attention_gain, attention_shift)
    normed = normed_full.astype(jnp.bfloat16)
    query_pre = jnp.dot(normed, query_weight, preferred_element_type=jnp.float32) + query_bias
    keyval_pre = jnp.dot(normed, keyval_weight, preferred_element_type=jnp.float32) + keyval_bias
    cos_table, sin_table = rotary_tables(positions)
    queries = rotate(
        query_pre.reshape(rows, local_len, HEADS, HEAD_DIM),
        cos_table[:, None, :],
        sin_table[:, None, :],
    ).astype(jnp.bfloat16)
    queries = queries.transpose(0, 2, 1, 3).reshape(rows, HEADS * local_len, HEAD_DIM)
    key_part = keyval_pre[:, :HEAD_DIM].reshape(rows, local_len, HEAD_DIM)
    value_part = keyval_pre[:, HEAD_DIM:].reshape(rows, local_len, HEAD_DIM)
    keyval_local = jnp.concatenate(
        [rotate(key_part, cos_table, sin_table), value_part], axis=-1
    ).astype(jnp.bfloat16)
    keyval_all, segment_all = (
        lax.all_gather(keyval_local, "seq", axis=1, tiled=True),
        lax.all_gather(segment_ids, "seq", axis=1, tiled=True),
    )

    def scores_of(query_rows, key_rows, segment_row, segment_keys):
        scores = contract_cols(query_rows, key_rows) * score_scale
        allowed = (positions[:, None] >= key_positions[None, :]) & (
            segment_row[:, None] == segment_keys[None, :]
        )
        scores = scores.reshape(HEADS, local_len, full_len)
        return jnp.where(allowed[None], scores, negative)

    def forward_row(pieces):
        query_rows, keyval_row, segment_row, segment_keys = pieces
        scores = scores_of(query_rows, keyval_row[:, :HEAD_DIM], segment_row, segment_keys)
        top_score = jnp.max(scores, axis=-1, keepdims=True)
        expanded = jnp.exp(scores - top_score)
        row_total = jnp.sum(expanded, axis=-1, keepdims=True)
        weights = (expanded / row_total).reshape(HEADS * local_len, full_len).astype(jnp.bfloat16)
        attended_row = jnp.dot(
            weights, keyval_row[:, HEAD_DIM:], preferred_element_type=jnp.float32
        ).astype(jnp.bfloat16)
        log_total = (top_score + jnp.log(row_total)).reshape(HEADS * local_len)
        return (attended_row, log_total)

    attended, log_totals = lax.map(forward_row, (queries, keyval_all, segment_ids, segment_all))
    attended_flat = (
        attended.reshape(rows, HEADS, local_len, HEAD_DIM)
        .transpose(0, 2, 1, 3)
        .reshape(tok_count, width)
    )
    attn_out = jnp.dot(attended_flat, out_weight, preferred_element_type=jnp.float32) + out_bias
    dense_full, dense_pull = jax.vjp(layer_norm, inputs, dense_gain, dense_shift)
    dense_in = dense_full.astype(jnp.bfloat16)
    hidden = jnp.dot(dense_in, up_weight, preferred_element_type=jnp.float32) + up_bias
    activated_full, gelu_pull = jax.vjp(partial(jax.nn.gelu, approximate=False), hidden)
    activated = activated_full.astype(jnp.bfloat16)
    dense_out = jnp.dot(activated, down_weight, preferred_element_type=jnp.float32) + down_bias
    layer_out = (
        (inputs + valid_rows * (attn_out + dense_out))
        .astype(jnp.bfloat16)
        .reshape(rows, local_len, width)
    )
    upstream = out_cotangent.astype(jnp.float32).reshape(tok_count, width)
    branch_full = valid_rows * upstream
    branch_grad = branch_full.astype(jnp.bfloat16)
    branch_sum = jnp.sum(branch_full, axis=0)
    grad_out_weight = contract_rows(attended_flat, branch_grad)
    grad_down_weight = contract_rows(activated, branch_grad)
    (grad_hidden_full,) = gelu_pull(contract_cols(branch_grad, down_weight))
    grad_hidden = grad_hidden_full.astype(jnp.bfloat16)
    grad_up_weight = contract_rows(dense_in, grad_hidden)
    grad_up_bias = jnp.sum(grad_hidden.astype(jnp.float32), axis=0)
    grad_dense_in = contract_cols(grad_hidden, up_weight)
    dense_back, grad_dense_gain, grad_dense_shift = dense_pull(grad_dense_in)
    grad_attended = contract_cols(branch_grad, out_weight).astype(jnp.bfloat16)
    grad_attended = (
        grad_attended.reshape(rows, local_len, HEADS, HEAD_DIM)
        .transpose(0, 2, 1, 3)
        .reshape(rows, HEADS * local_len, HEAD_DIM)
    )
    keyval_back, segment_back = (
        lax.all_gather(keyval_local, "seq", axis=1, tiled=True),
        lax.all_gather(segment_ids, "seq", axis=1, tiled=True),
    )

    def backward_row(pieces):
        query_rows, keyval_row, segment_row, segment_keys, log_row, grad_rows = pieces
        key_rows = keyval_row[:, :HEAD_DIM]
        value_rows = keyval_row[:, HEAD_DIM:]
        scores = scores_of(query_rows, key_rows, segment_row, segment_keys)
        probs = jnp.exp(scores - log_row.reshape(HEADS, local_len, 1)).reshape(
            HEADS * local_len, full_len
        )
        grad_probs = contract_cols(grad_rows, value_rows)
        inner = jnp.sum(probs * grad_probs, axis=-1, keepdims=True)
        grad_scores = (probs * (grad_probs - inner)).astype(jnp.bfloat16)
        grad_query_rows = (
            jnp.dot(grad_scores, key_rows, preferred_element_type=jnp.float32) * score_scale
        )
        grad_key_rows = contract_rows(grad_scores, query_rows) * score_scale
        grad_value_rows = contract_rows(probs.astype(jnp.bfloat16), grad_rows)
        return (grad_query_rows, jnp.concatenate([grad_key_rows, grad_value_rows], axis=-1))

    grad_queries, keyval_terms = lax.map(
        backward_row, (queries, keyval_back, segment_ids, segment_back, log_totals, grad_attended)
    )
    keyval_grad = lax.psum_scatter(
        keyval_terms.astype(jnp.bfloat16), "seq", scatter_dimension=1, tiled=True
    ).astype(jnp.float32) + keyval_cotangent.astype(jnp.float32)
    grad_key_pre = unrotate(keyval_grad[..., :HEAD_DIM], cos_table, sin_table)
    grad_keyval_pre = (
        jnp.concatenate([grad_key_pre, keyval_grad[..., HEAD_DIM:]], axis=-1)
        .reshape(tok_count, 2 * HEAD_DIM)
        .astype(jnp.bfloat16)
    )
    grad_queries = grad_queries.reshape(rows, HEADS, local_len, HEAD_DIM).transpose(0, 2, 1, 3)
    grad_query_pre = (
        unrotate(grad_queries, cos_table[:, None, :], sin_table[:, None, :])
        .reshape(tok_count, width)
        .astype(jnp.bfloat16)
    )
    grad_query_weight = contract_rows(normed, grad_query_pre)
    grad_query_bias = jnp.sum(grad_query_pre.astype(jnp.float32), axis=0)
    grad_keyval_weight = contract_rows(normed, grad_keyval_pre)
    grad_keyval_bias = jnp.sum(grad_keyval_pre.astype(jnp.float32), axis=0)
    grad_normed = contract_cols(grad_query_pre, query_weight) + contract_cols(
        grad_keyval_pre, keyval_weight
    )
    attention_back, grad_attention_gain, grad_attention_shift = attention_pull(grad_normed)
    grad_tokens = (
        (upstream + attention_back + dense_back)
        .astype(jnp.bfloat16)
        .reshape(rows, local_len, width)
    )
    local_grads = (
        grad_query_weight,
        grad_query_bias,
        grad_keyval_weight,
        grad_keyval_bias,
        grad_out_weight,
        branch_sum,
        grad_up_weight,
        grad_up_bias,
        grad_down_weight,
        branch_sum,
        grad_attention_gain,
        grad_attention_shift,
        grad_dense_gain,
        grad_dense_shift,
    )
    shares = (
        lax.psum_scatter(
            local_grads[0].astype(jnp.bfloat16), "seq", scatter_dimension=0, tiled=True
        ).astype(jnp.float32),
        lax.psum_scatter(
            local_grads[1].astype(jnp.bfloat16), "seq", scatter_dimension=0, tiled=True
        ).astype(jnp.float32),
        lax.psum_scatter(
            local_grads[2].astype(jnp.bfloat16), "seq", scatter_dimension=0, tiled=True
        ).astype(jnp.float32),
        lax.psum_scatter(
            local_grads[3].astype(jnp.bfloat16), "seq", scatter_dimension=0, tiled=True
        ).astype(jnp.float32),
        lax.psum_scatter(
            local_grads[4].astype(jnp.bfloat16), "seq", scatter_dimension=0, tiled=True
        ).astype(jnp.float32),
        lax.psum_scatter(
            local_grads[5].astype(jnp.bfloat16), "seq", scatter_dimension=0, tiled=True
        ).astype(jnp.float32),
        lax.psum_scatter(
            local_grads[6].astype(jnp.bfloat16), "seq", scatter_dimension=0, tiled=True
        ).astype(jnp.float32),
        lax.psum_scatter(
            local_grads[7].astype(jnp.bfloat16), "seq", scatter_dimension=0, tiled=True
        ).astype(jnp.float32),
        lax.psum_scatter(
            local_grads[8].astype(jnp.bfloat16), "seq", scatter_dimension=0, tiled=True
        ).astype(jnp.float32),
        lax.psum_scatter(
            local_grads[9].astype(jnp.bfloat16), "seq", scatter_dimension=0, tiled=True
        ).astype(jnp.float32),
        lax.psum_scatter(
            local_grads[10].astype(jnp.bfloat16), "seq", scatter_dimension=0, tiled=True
        ).astype(jnp.float32),
        lax.psum_scatter(
            local_grads[11].astype(jnp.bfloat16), "seq", scatter_dimension=0, tiled=True
        ).astype(jnp.float32),
        lax.psum_scatter(
            local_grads[12].astype(jnp.bfloat16), "seq", scatter_dimension=0, tiled=True
        ).astype(jnp.float32),
        lax.psum_scatter(
            local_grads[13].astype(jnp.bfloat16), "seq", scatter_dimension=0, tiled=True
        ).astype(jnp.float32),
    )
    totals = (
        lax.psum(shares[0].astype(jnp.bfloat16), "batch").astype(jnp.float32),
        lax.psum(shares[1].astype(jnp.bfloat16), "batch").astype(jnp.float32),
        lax.psum(shares[2].astype(jnp.bfloat16), "batch").astype(jnp.float32),
        lax.psum(shares[3].astype(jnp.bfloat16), "batch").astype(jnp.float32),
        lax.psum(shares[4].astype(jnp.bfloat16), "batch").astype(jnp.float32),
        lax.psum(shares[5].astype(jnp.bfloat16), "batch").astype(jnp.float32),
        lax.psum(shares[6].astype(jnp.bfloat16), "batch").astype(jnp.float32),
        lax.psum(shares[7].astype(jnp.bfloat16), "batch").astype(jnp.float32),
        lax.psum(shares[8].astype(jnp.bfloat16), "batch").astype(jnp.float32),
        lax.psum(shares[9].astype(jnp.bfloat16), "batch").astype(jnp.float32),
        lax.psum(shares[10].astype(jnp.bfloat16), "batch").astype(jnp.float32),
        lax.psum(shares[11].astype(jnp.bfloat16), "batch").astype(jnp.float32),
        lax.psum(shares[12].astype(jnp.bfloat16), "batch").astype(jnp.float32),
        lax.psum(shares[13].astype(jnp.bfloat16), "batch").astype(jnp.float32),
    )
    return (
        layer_out,
        keyval_local,
        grad_tokens,
        totals[0],
        totals[1],
        totals[2],
        totals[3],
        totals[4],
        totals[5],
        totals[6],
        totals[7],
        totals[8],
        totals[9],
        totals[10],
        totals[11],
        totals[12],
        totals[13],
    )


def solution(mesh):
    placed = (
        P("batch", "seq", None),
        P("batch", "seq"),
        P(),
        P(),
        P(),
        P(),
        P(),
        P(),
        P(),
        P(),
        P(),
        P(),
        P(),
        P(),
        P(),
        P(),
        P("batch", "seq", None),
        P("batch", "seq", None),
    )
    return jax.shard_map(
        local,
        mesh=mesh,
        in_specs=placed,
        out_specs=(
            P("batch", "seq", None),
            P("batch", "seq", None),
            P("batch", "seq", None),
            P("seq", None),
            P("seq"),
            P("seq", None),
            P("seq"),
            P("seq", None),
            P("seq"),
            P("seq", None),
            P("seq"),
            P("seq", None),
            P("seq"),
            P("seq"),
            P("seq"),
            P("seq"),
            P("seq"),
        ),
        check_vma=False,
    )
```

profile of v0, /device:TPU:0, one launch (start us, length us, event | category | flops | bytes accessed | tf_op | source)
XLA Modules:
  0.0 1870.4 jit_solution(16724395352428913385)
XLA Ops:
  37.2 64.2 %multiply_convert_fusion.1 = (bf16[2048,3072]{1,0:T(8,128)(2,1)}, f32[2048,3072]{1,0:T(8,128)}, f32[2048,3072]{1,0:T(8,128)}) fusion(f32[3072]{0:T(1024)S(1)} %copy-done.55, bf16[2048,768]{1,0:T(8,128)(2,1)S(1)} %copy-done.14, bf16[768,3072]{1,0:T(8,128)(2,1)} %param.30), kind=kOutput, calls=%fused_computation.65 | convolution fusion | flops 10078912512 | bytes 70791168 | tf_op jit(solution)/shard_map/dot_general | solution.py:152
  101.4 33.7 %fusion.92 = (bf16[3072]{0:T(1024)(128)(2,1)}, bf16[2048,3072]{1,0:T(8,128)(2,1)}) fusion(f32[2048,3072]{1,0:T(8,128)} %get-tuple-element.315, bf16[2048,768]{1,0:T(8,128)(2,1)} %fusion.52, bf16[3072,768]{1,0:T(8,128)(2,1)} %param.32, f32[2048,3072]{1,0:T(8,128)} %get-tuple-element.346, f32[3072]{0:T(1024)S(1)} %copy-done.55), kind=kOutput, calls=%fused_computation.167 | convolution fusion | flops 9764336640 | bytes 70797312 | tf_op jit(solution)/shard_map/dot_general | solution.py:67
  135.1 15.5 convolution_convert_fusion.1
  150.7 15.4 convolution_convert_fusion
  187.7 34.6 %all_gather.8 = s32[8,2048]{1,0:T(8,128)} all-gather(s32[8,256]{1,0:T(8,128)S(1)} %copy-done.37), channel_id=1, replica_groups=mesh['batch'=4,'seq'=8] {'seq'}, dimensions={1}, use_global_device_ids=true | all-gather | bytes 73728 | tf_op jit(solution)/shard_map/all_gather | solution.py:119
  258.9 477.6 %while.26 = (s32[]{:T(128)}, bf16[8,3072,64]{1,2,0:T(8,128)(2,1)}, f32[8,3072]{1,0:T(8,128)}, s32[8,256]{1,0:T(8,128)S(1)}, s32[8,2048]{1,0:T(8,128)}, /*index=5...) while((s32[]{:T(128)}, bf16[8,3072,64]{1,2,0:T(8,128)(2,1)}, ...), condition=%wide.region_5.6_spmd.clone, body=%wide.region_2.5_spmd.clone.sunk | while | flops 1687876864 | bytes 142891168 | solution.py:143
  304.5 15.0 fusion.149
  483.6 14.7 fusion.149
  543.1 14.7 fusion.149
  736.5 749.6 %while.27 = (s32[]{:T(128)}, f32[8,3072,64]{1,2,0:T(8,128)}, bf16[8,2048,128]{2,1,0:T(8,128)(2,1)}, s32[8,256]{1,0:T(8,128)S(1)}, s32[8,2048]{1,0:T(8,128)}, /*i...) while((s32[]{:T(128)}, f32[8,3072,64]{1,2,0:T(8,128)}, ...), condition=%wide.region_8.9_spmd.clone, body=%wide.region_6.8_spmd.clone.sunk | while | flops 4086232320 | bytes 275607712 | solution.py:202
  763.7 18.7 multiply_reduce_fusion.2
  782.4 16.9 multiply_convert_fusion.3
  857.3 18.7 %multiply_reduce_fusion.2 = (f32[3072]{0:T(1024)S(1)}, f32[3072,2048]{0,1:T(8,128)}) fusion(f32[3072,2048]{0,1:T(8,128)} %fusion.158, f32[3072]{0:T(1024)S(1)} %bitcast.247, pred[3072,2048]{0,1:T(32,128)(4,1)} %copy.173, bf16[2048,128]{1,0:T(8,128)(2,1)S(1)} %dynamic-slice_bitcast_fusion.5, bf16[8,3072,64]{2,1,0:T(8,128)(2,1)} %get-tuple-element.527, ...), kind=kOutput, calls=%fused_computation.29.clone.1 | convolution fusion | flops 836760576 | bytes 57958912 | tf_op jit(solution)/shard_map/while/body/eval_jaxpr/dot_general | solution.py:67
  876.0 16.9 multiply_convert_fusion.3
  950.9 18.7 multiply_reduce_fusion.2
  969.6 16.9 multiply_convert_fusion.3
  1044.4 18.8 %multiply_reduce_fusion.2 = (f32[3072]{0:T(1024)S(1)}, f32[3072,2048]{0,1:T(8,128)}) fusion(f32[3072,2048]{0,1:T(8,128)} %fusion.158, f32[3072]{0:T(1024)S(1)} %bitcast.247, pred[3072,2048]{0,1:T(32,128)(4,1)} %copy.173, bf16[2048,128]{1,0:T(8,128)(2,1)S(1)} %dynamic-slice_bitcast_fusion.5, bf16[8,3072,64]{2,1,0:T(8,128)(2,1)} %get-tuple-element.527, ...), kind=kOutput, calls=%fused_computation.29.clone.1 | convolution fusion | flops 836760576 | bytes 57958912 | tf_op jit(solution)/shard_map/while/body/eval_jaxpr/dot_general | solution.py:67
  1063.2 16.9 multiply_convert_fusion.3
  1138.0 18.8 %multiply_reduce_fusion.2 = (f32[3072]{0:T(1024)S(1)}, f32[3072,2048]{0,1:T(8,128)}) fusion(f32[3072,2048]{0,1:T(8,128)} %fusion.158, f32[3072]{0:T(1024)S(1)} %bitcast.247, pred[3072,2048]{0,1:T(32,128)(4,1)} %copy.173, bf16[2048,128]{1,0:T(8,128)(2,1)S(1)} %dynamic-slice_bitcast_fusion.5, bf16[8,3072,64]{2,1,0:T(8,128)(2,1)} %get-tuple-element.527, ...), kind=kOutput, calls=%fused_computation.29.clone.1 | convolution fusion | flops 836760576 | bytes 57958912 | tf_op jit(solution)/shard_map/while/body/eval_jaxpr/dot_general | solution.py:67
  1156.8 16.9 multiply_convert_fusion.3
  1231.7 18.9 %multiply_reduce_fusion.2 = (f32[3072]{0:T(1024)S(1)}, f32[3072,2048]{0,1:T(8,128)}) fusion(f32[3072,2048]{0,1:T(8,128)} %fusion.158, f32[3072]{0:T(1024)S(1)} %bitcast.247, pred[3072,2048]{0,1:T(32,128)(4,1)} %copy.173, bf16[2048,128]{1,0:T(8,128)(2,1)S(1)} %dynamic-slice_bitcast_fusion.5, bf16[8,3072,64]{2,1,0:T(8,128)(2,1)} %get-tuple-element.527, ...), kind=kOutput, calls=%fused_computation.29.clone.1 | convolution fusion | flops 836760576 | bytes 57958912 | tf_op jit(solution)/shard_map/while/body/eval_jaxpr/dot_general | solution.py:67
  1250.6 16.9 multiply_convert_fusion.3
  1325.6 18.8 %multiply_reduce_fusion.2 = (f32[3072]{0:T(1024)S(1)}, f32[3072,2048]{0,1:T(8,128)}) fusion(f32[3072,2048]{0,1:T(8,128)} %fusion.158, f32[3072]{0:T(1024)S(1)} %bitcast.247, pred[3072,2048]{0,1:T(32,128)(4,1)} %copy.173, bf16[2048,128]{1,0:T(8,128)(2,1)S(1)} %dynamic-slice_bitcast_fusion.5, bf16[8,3072,64]{2,1,0:T(8,128)(2,1)} %get-tuple-element.527, ...), kind=kOutput, calls=%fused_computation.29.clone.1 | convolution fusion | flops 836760576 | bytes 57958912 | tf_op jit(solution)/shard_map/while/body/eval_jaxpr/dot_general | solution.py:67
  1344.3 16.9 multiply_convert_fusion.3
  1419.2 18.8 %multiply_reduce_fusion.2 = (f32[3072]{0:T(1024)S(1)}, f32[3072,2048]{0,1:T(8,128)}) fusion(f32[3072,2048]{0,1:T(8,128)} %fusion.158, f32[3072]{0:T(1024)S(1)} %bitcast.247, pred[3072,2048]{0,1:T(32,128)(4,1)} %copy.173, bf16[2048,128]{1,0:T(8,128)(2,1)S(1)} %dynamic-slice_bitcast_fusion.5, bf16[8,3072,64]{2,1,0:T(8,128)(2,1)} %get-tuple-element.527, ...), kind=kOutput, calls=%fused_computation.29.clone.1 | convolution fusion | flops 836760576 | bytes 57958912 | tf_op jit(solution)/shard_map/while/body/eval_jaxpr/dot_general | solution.py:67
  1438.0 16.9 multiply_convert_fusion.3
  1536.3 43.2 %reduce-scatter.9.cloned.1.call-done = bf16[96,768]{1,0:T(8,128)(2,1)} async-done(((bf16[768,768]{1,0:T(8,128)(2,1)}), bf16[96,768]{1,0:T(8,128)(2,1)}) %reduce-scatter.9.cloned.1.call-update) | async-done | bytes 147472 | tf_op jit(solution)/shard_map/reduce_scatter | solution.py:250
  1579.6 66.8 %reduce-scatter.13.cloned.1.call-done = bf16[96,768]{1,0:T(8,128)(2,1)} async-done(((bf16[768,768]{1,0:T(8,128)(2,1)}), bf16[96,768]{1,0:T(8,128)(2,1)}) %reduce-scatter.13.cloned.1.call-update) | async-done | bytes 147472 | tf_op jit(solution)/shard_map/reduce_scatter | solution.py:262
  1649.7 16.2 fusion.95
  1676.4 14.8 fusion.78
  1698.8 82.9 %reduce-scatter.7.cloned.1.call-done = bf16[8,256,128]{2,1,0:T(8,128)(2,1)} async-done(((bf16[8,2048,128]{2,1,0:T(8,128)(2,1)}), bf16[8,256,128]{2,1,0:T(8,128)(2,1)}) %reduce-scatter.7.cloned.1.call-update) | async-done | bytes 524304 | tf_op jit(solution)/shard_map/reduce_scatter | solution.py:205
  1805.7 35.9 %all-reduce.8 = (bf16[768]{0:T(1024)(128)(2,1)S(1)}, bf16[128]{0:T(256)(128)(2,1)S(1)}, bf16[768]{0:T(1024)(128)(2,1)S(1)}, bf16[3072]{0:T(1024)(128)(2,1)S(1)},...) all-reduce(bf16[768]{0:T(1024)(128)(2,1)S(1)} %reduce_sum.172, ...), channel_id=4, replica_groups=mesh['batch'=4,'seq'=8] {'seq'}, use_global_device_ids=true, to_apply=%region_17.18.clone | all-reduce | flops 7808 | bytes 31232
  (488 shorter events, 1097.8 us)
Async XLA Ops:
  7.2 159.2 %copy-start = (bf16[768,768]{1,0:T(8,128)(2,1)S(1)}, bf16[768,768]{1,0:T(8,128)(2,1)}, u32[]{:S(2)}) copy-start(bf16[768,768]{1,0:T(8,128)(2,1)} %param.24) | copy-start | bytes 3538948
  7.2 251.7 %all-gather.2.cloned.1.call-start = ((), (), s32[]{:S(2)}) async-start(), calls=%async_computation.6 | async-start | bytes 4718592 | tf_op jit(solution)/shard_map/all_gather | solution.py:118
  19.7 12.1 copy-start.36
  22.0 15.2 copy-start.30
  22.5 14.6 copy-start.16
  22.7 14.5 copy-start.18
  31.3 1505.0 %reduce-scatter.15.cloned.1.call-start = ((), (), s32[]{:S(2)}) async-start(), calls=%async_computation.11 | async-start | bytes 5308416 | tf_op jit(solution)/shard_map/reduce_scatter | solution.py:268
  150.6 1385.7 %reduce-scatter.17.cloned.1.call-start = ((), (), s32[]{:S(2)}) async-start(), calls=%async_computation.12 | async-start | bytes 5308416 | tf_op jit(solution)/shard_map/reduce_scatter | solution.py:274
  150.7 15.7 copy-start.56
  166.1 1413.4 %reduce-scatter.9.cloned.1.call-start = ((), (), s32[]{:S(2)}) async-start(), calls=%async_computation.8 | async-start | bytes 1327104 | tf_op jit(solution)/shard_map/reduce_scatter | solution.py:250
  277.2 14.0 copy-start.2
  337.3 14.0 copy-start.2
  397.0 13.8 copy-start.2
  456.6 13.8 copy-start.2
  516.1 13.8 copy-start.2
  575.6 13.8 copy-start.2
  635.2 13.8 copy-start.2
  694.7 13.8 copy-start.2
  1514.4 132.0 %reduce-scatter.13.cloned.1.call-start = ((), (), s32[]{:S(2)}) async-start(), calls=%async_computation.10 | async-start | bytes 1327104 | tf_op jit(solution)/shard_map/reduce_scatter | solution.py:262
  1536.2 111.0 %copy-start.59 = (u32[32]{0:T(128)S(1)}, u32[32]{0:T(128)}, u32[]{:S(2)}) copy-start(u32[32]{0:T(128)} %constant.149) | copy-start | bytes 388
  1536.2 154.9 %all-reduce.13.cloned.1.call-start = ((), (), s32[]{:S(2)}) async-start(), calls=%async_computation.13 | async-start | bytes 2949120 | tf_op jit(solution)/shard_map/psum | solution.py:294
  1646.4 135.3 %reduce-scatter.7.cloned.1.call-start = ((), (), s32[]{:S(2)}) async-start(), calls=%async_computation.7 | async-start | bytes 4718592 | tf_op jit(solution)/shard_map/reduce_scatter | solution.py:205
  1647.1 200.6 %reduce-scatter.11.cloned.1.call-start = ((), (), s32[]{:S(2)}) async-start(), calls=%async_computation.9 | async-start | bytes 221184 | tf_op jit(solution)/shard_map/reduce_scatter | solution.py:256
  1666.1 10.2 slice-start.2
  1676.3 105.3 %copy-start.22 = (bf16[8,256,128]{2,1,0:T(8,128)(2,1)S(1)}, bf16[8,256,128]{2,1,0:T(8,128)(2,1)}, u32[]{:S(2)}) copy-start(bf16[8,256,128]{2,1,0:T(8,128)(2,1)} %param.39) | copy-start | bytes 1572868
  1691.1 91.9 %copy-start.17 = (f32[256,8]{1,0:T(8,128)S(1)}, f32[256,8]{1,0:T(8,128)}, u32[]{:S(2)}) copy-start(f32[256,8]{1,0:T(8,128)} %copy-done.16) | copy-start | bytes 24580
  1691.1 91.9 %copy-start.19 = (f32[256,8]{1,0:T(8,128)S(1)}, f32[256,8]{1,0:T(8,128)}, u32[]{:S(2)}) copy-start(f32[256,8]{1,0:T(8,128)} %copy-done.18) | copy-start | bytes 24580
  1698.8 88.0 %copy-start.21 = (bf16[768,128]{1,0:T(8,128)(2,1)S(1)}, bf16[768,128]{1,0:T(8,128)(2,1)}, u32[]{:S(2)}) copy-start(bf16[768,128]{1,0:T(8,128)(2,1)} %param.26) | copy-start | bytes 589828
  1698.8 88.0 %copy-start.24 = (f32[1,2,8,128]{3,1,2,0:T(2,128)S(1)}, f32[1,2,8,128]{3,1,2,0:T(2,128)}, u32[]{:S(2)}) copy-start(f32[1,2,8,128]{3,1,2,0:T(2,128)} %copy-done.23) | copy-start | bytes 24580
  1698.8 88.0 %copy-start.35 = (f32[768]{0:T(1024)S(1)}, f32[768]{0:T(1024)}, u32[]{:S(2)}) copy-start(f32[768]{0:T(1024)} %param.34) | copy-start | bytes 9220
  1698.8 88.0 %copy-start.43 = (f32[768]{0:T(1024)S(1)}, f32[768]{0:T(1024)}, u32[]{:S(2)}) copy-start(f32[768]{0:T(1024)} %param.36) | copy-start | bytes 9220
  1785.0 10.1 slice-start
  (55 other events, 289.0 us)
Sparse Core Ops, SparseCore 0:
  31.4 76.0 all-gather.1
  150.8 99.0 reduce-scatter.14
  253.5 95.0 reduce-scatter.16
  1514.5 65.0 reduce-scatter.8
  1583.4 62.9 reduce-scatter.12
  1648.8 40.7 all-reduce.12
  1693.7 87.9 reduce-scatter.6
  1786.9 60.8 reduce-scatter.10
where the time goes:
time: 1880 us; the launch traced here: 1870 us
  matrix products  860 us (46%)
  local copies, waits for them, and re-layouts  411 us (22%)
  other arithmetic  298 us (16%)
  waiting for transfers between devices  199 us (11%)
  blocking collectives  81.4 us (4%)
    dot_general x29, matrix products, contract_cols(): lax.dot_general(left_side, right_side, (((1,), (1,)), ((), ())), preferre...  411 us
    broadcast_in_dim x32, local copies, waits for them, and re-layouts, scores_of(): return jnp.where(allowed[None], scores, negative)  230 us
    dot_general x21, matrix products, contract_rows(): lax.dot_general(left_side, right_side, (((0,), (0,)), ((), ())), preferre...  178 us
    convert_element_type x8, other arithmetic, backward_row(): grad_scores = (probs * (grad_probs - inner)).astype(jnp.bfloat16)  136 us
    dot_general x8, matrix products, forward_row(): jnp.dot(weights, keyval_row[:, HEAD_DIM:], preferred_element_type=jnp.flo...  118 us
    reduce_sum x8, other arithmetic, forward_row(): row_total = jnp.sum(expanded, axis=-1, keepdims=True)  92.9 us
    reduce_scatter x1, waiting for transfers between devices, local(): lax.psum_scatter(keyval_terms.astype(jnp.bfloat16), 'seq', scatter_dimens...  82.9 us
    reduce_scatter x1, waiting for transfers between devices, local(): lax.psum_scatter(local_grads[4].astype(jnp.bfloat16), 'seq', scatter_dime...  66.8 us
  transfers between devices with their start and end apart: 8, of which 4 were waited for; matrix products, arithmetic and copies ran while one was open for 80% of the time, Pallas kernels for 0%

commit v1 on v0

--- a/solution.py
+++ b/solution.py
@@ -3,11 +3,15 @@
 import jax
 import jax.numpy as jnp
 from jax import lax
+from jax.experimental import pallas as pl
+from jax.experimental.pallas import tpu as pltpu
 from jax.sharding import PartitionSpec as P
 
 HEADS = 12
 HEAD_DIM = 64
 ROT = 16
+f32 = jnp.float32
+bf16 = jnp.bfloat16
 
 
 epsilon = 1e-05
@@ -69,7 +73,143 @@
     )
 
 
-def local(
+LOG2E=1.4426950408889634
+NEG=-1e30
+def nn(a,b): return lax.dot_general(a,b,(((1,),(0,)),((),())),preferred_element_type=f32)
+def nt(a,b): return lax.dot_general(a,b,(((1,),(1,)),((),())),preferred_element_type=f32)
+
+def attn_kernel(first_ref, sidx_ref, q_ref, do_ref, kv_ref, start_ref, cos_ref, sin_ref,
+                att_ref, gq_ref, dkv_ref,
+                qz, dz, p_s, m_s, bias_s, o_s, mx, ls, dq_s, dc_s, inn_s, ds_s, ic_s, *, blk, nblk):
+    r = pl.program_id(0)
+    L = HEADS*blk
+    e = sidx_ref[0]
+    n = e - first_ref[r] + 1
+    qz[0:HEAD_DIM,:] = q_ref[0]
+    qz[HEAD_DIM:,:] = jnp.zeros((HEAD_DIM,L),bf16)
+    dz[0:HEAD_DIM,:] = jnp.zeros((HEAD_DIM,L),bf16)
+    mx[...] = jnp.full((1,L),NEG,f32)
+    ls[...] = jnp.zeros((1,L),f32)
+    o_s[...] = jnp.zeros((HEAD_DIM,L),f32)
+    dq_s[...] = jnp.zeros((HEAD_DIM,L),f32)
+    start = start_ref[0]
+    qpos = e*blk + lax.broadcasted_iota(jnp.int32,(1,blk),1)
+    krow = lax.broadcasted_iota(jnp.int32,(blk,blk),0)
+
+    @pl.loop(0, nblk)
+    def _(j):
+        @pl.when((j < first_ref[r]) | (j > e))
+        def _():
+            dkv_ref[0,j] = jnp.zeros((blk,2*HEAD_DIM),bf16)
+
+    @pl.loop(0, n)
+    def _(jj):
+        j = e - jj
+        kvj = kv_ref[0, pl.ds(pl.multiple_of(j*blk,blk),blk), :]
+        vt = kvj.T[HEAD_DIM:,:]
+        kpos = j*blk + krow
+        bias_s[...] = jnp.where((kpos>=start)&(kpos<=qpos), 0.0, NEG)
+        def hsl(h): return slice(h*blk,(h+1)*blk)
+        sv = {}; pv = {}; av = {}
+        for h in range(HEADS+2):
+            if h < HEADS:
+                sv[h] = nn(kvj, qz[:,hsl(h)])
+            if 0 <= h-2 < HEADS:
+                g = h-2; hs = hsl(g)
+                o_s[:,hs] = o_s[:,hs]*av.pop(g) + nn(vt,pv.pop(g))
+            if 0 <= h-1 < HEADS:
+                g = h-1; hs = hsl(g)
+                s = sv.pop(g)*LOG2E + bias_s[...]
+                mo = mx[:,hs]
+                mn = jnp.maximum(mo, jnp.max(s,axis=0,keepdims=True))
+                p = jnp.exp2(s-mn)
+                a = jnp.exp2(mo-mn)
+                ls[:,hs] = ls[:,hs]*a + jnp.sum(p,axis=0,keepdims=True)
+                pb = p.astype(bf16)
+                p_s[jj,:,hs] = pb
+                m_s[jj,:,hs] = mn
+                mx[:,hs] = mn
+                pv[g]=pb; av[g]=a
+
+    inv = 1.0/ls[...]
+    o = o_s[...]*inv
+    for h in range(HEADS):
+        att_ref[0, h*HEAD_DIM:(h+1)*HEAD_DIM, :] = o[:, h*blk:(h+1)*blk].astype(bf16)
+    do = do_ref[0].astype(f32)
+    inn_s[...] = jnp.sum(o*do,axis=0,keepdims=True)
+    ls[...] = inv
+
+    @pl.loop(0, n)
+    def _(jj):
+        j = e - jj
+        kvj = kv_ref[0, pl.ds(pl.multiple_of(j*blk,blk),blk), :]
+        kt = kvj.T[:HEAD_DIM,:]
+        def hsl(h): return slice(h*blk,(h+1)*blk)
+        c = jnp.exp2(m_s[jj]-mx[...])*ls[...]
+        dc_s[...] = (do_ref[0].astype(f32)*c).astype(bf16)
+        dz[HEAD_DIM:,:] = dc_s[...]
+        ic_s[...] = inn_s[...]*c
+        dpv = {}; dsv = {}
+        for h in range(HEADS+2):
+            if h < HEADS:
+                dpv[h] = nn(kvj, dz[:,hsl(h)])
+            if 0 <= h-2 < HEADS:
+                g = h-2; hs = hsl(g)
+                dq_s[:,hs] = dq_s[:,hs] + nn(kt, dsv.pop(g))
+            if 0 <= h-1 < HEADS:
+                g = h-1; hs = hsl(g)
+                pb = p_s[jj,:,hs]
+                ds = (pb.astype(f32)*(dpv.pop(g)-ic_s[:,hs])).astype(bf16)
+                ds_s[:,hs] = ds
+                dsv[g] = ds
+        dv = nt(p_s[jj], dc_s[...])
+        dk = nt(ds_s[...], qz[0:HEAD_DIM,:])
+        dkv_ref[0,j] = jnp.concatenate([dk,dv],axis=1).astype(bf16)
+
+    cos = cos_ref[...]; sin = sin_ref[...]
+    for h in range(HEADS):
+        g = dq_s[:, h*blk:(h+1)*blk]*(HEAD_DIM**-0.5)
+        a, b = g[0:8], g[8:16]
+        gq_ref[0, h*HEAD_DIM:(h+1)*HEAD_DIM, :] = jnp.concatenate([a*cos+b*sin, b*cos-a*sin, g[16:]],axis=0).astype(bf16)
+
+def attention(first, sidx, qT, doT, kv, start, cosT, sinT):
+    rows, _, L = qT.shape
+    blk = L//HEADS
+    length = kv.shape[1]; nblk = length//blk
+    gs = pltpu.PrefetchScalarGridSpec(
+        num_scalar_prefetch=2, grid=(rows,),
+        in_specs=[
+            pl.BlockSpec((1,HEAD_DIM,L),lambda r,*_:(r,0,0)),
+            pl.BlockSpec((1,HEAD_DIM,L),lambda r,*_:(r,0,0)),
+            pl.BlockSpec((1,length,2*HEAD_DIM),lambda r,*_:(r,0,0)),
+            pl.BlockSpec((1,1,blk),lambda r,*_:(r,0,0)),
+            pl.BlockSpec((8,blk),lambda r,*_:(0,0)),
+            pl.BlockSpec((8,blk),lambda r,*_:(0,0)),
+        ],
+        out_specs=[
+            pl.BlockSpec((1,HEADS*HEAD_DIM,blk),lambda r,*_:(r,0,0)),
+            pl.BlockSpec((1,HEADS*HEAD_DIM,blk),lambda r,*_:(r,0,0)),
+            pl.BlockSpec((1,nblk,blk,2*HEAD_DIM),lambda r,*_:(r,0,0,0)),
+        ],
+        scratch_shapes=[
+            pltpu.VMEM((2*HEAD_DIM,L),bf16), pltpu.VMEM((2*HEAD_DIM,L),bf16),
+            pltpu.VMEM((nblk,blk,L),bf16), pltpu.VMEM((nblk,1,L),f32),
+            pltpu.VMEM((blk,blk),f32), pltpu.VMEM((HEAD_DIM,L),f32),
+            pltpu.VMEM((1,L),f32), pltpu.VMEM((1,L),f32),
+            pltpu.VMEM((HEAD_DIM,L),f32), pltpu.VMEM((HEAD_DIM,L),bf16), pltpu.VMEM((1,L),f32), pltpu.VMEM((blk,L),bf16), pltpu.VMEM((1,L),f32),
+        ])
+    return pl.pallas_call(
+        partial(attn_kernel, blk=blk, nblk=nblk),
+        out_shape=[jax.ShapeDtypeStruct((rows,HEADS*HEAD_DIM,blk),bf16),
+                   jax.ShapeDtypeStruct((rows,HEADS*HEAD_DIM,blk),bf16),
+                   jax.ShapeDtypeStruct((rows,nblk,blk,2*HEAD_DIM),bf16)],
+        grid_spec=gs,
+        compiler_params=pltpu.CompilerParams(vmem_limit_bytes=56*2**20),
+        name="attention",
+    )(first, sidx, qT, doT, kv, start, cosT, sinT)
+
+
+def local_plain(
     tokens,
     segment_ids,
     query_weight,
@@ -327,6 +467,229 @@
     )
 
 
+def local(
+    tokens,
+    segment_ids,
+    query_weight,
+    query_bias,
+    keyval_weight,
+    keyval_bias,
+    out_weight,
+    out_bias,
+    up_weight,
+    up_bias,
+    down_weight,
+    down_bias,
+    attention_gain,
+    attention_shift,
+    dense_gain,
+    dense_shift,
+    out_cotangent,
+    keyval_cotangent,
+):
+    rows, local_len, width = tokens.shape
+    full_len = local_len * lax.axis_size("seq")
+    tok_count = rows * local_len
+    offset = lax.axis_index("seq") * local_len
+    positions = offset + jnp.arange(local_len, dtype=jnp.int32)
+    score_scale = HEAD_DIM ** (-0.5)
+    inputs = tokens.astype(jnp.float32).reshape(tok_count, width)
+    valid_rows = (segment_ids >= 0).astype(jnp.float32).reshape(tok_count, 1)
+    normed_full, attention_pull = jax.vjp(layer_norm, inputs, attention_gain, attention_shift)
+    normed = normed_full.astype(jnp.bfloat16)
+    query_pre = jnp.dot(normed, query_weight, preferred_element_type=jnp.float32) + query_bias
+    keyval_pre = jnp.dot(normed, keyval_weight, preferred_element_type=jnp.float32) + keyval_bias
+    cos_table, sin_table = rotary_tables(positions)
+    queries = rotate(
+        query_pre.reshape(rows, local_len, HEADS, HEAD_DIM),
+        cos_table[:, None, :],
+        sin_table[:, None, :],
+    ).astype(jnp.bfloat16) * jnp.asarray(score_scale, jnp.bfloat16)
+    queries = queries.transpose(0, 3, 2, 1).reshape(rows, HEAD_DIM, HEADS * local_len)
+    key_part = keyval_pre[:, :HEAD_DIM].reshape(rows, local_len, HEAD_DIM)
+    value_part = keyval_pre[:, HEAD_DIM:].reshape(rows, local_len, HEAD_DIM)
+    keyval_local = jnp.concatenate(
+        [rotate(key_part, cos_table, sin_table), value_part], axis=-1
+    ).astype(jnp.bfloat16)
+    keyval_all, segment_all = (
+        lax.all_gather(keyval_local, "seq", axis=1, tiled=True),
+        lax.all_gather(segment_ids, "seq", axis=1, tiled=True),
+    )
+
+    order_all = jnp.where(segment_all < 0, 1 << 20, segment_all)
+    order_own = jnp.where(segment_ids < 0, 1 << 20, segment_ids)
+    start = jnp.sum(
+        (order_all[:, None, :] < order_own[:, :, None]).astype(jnp.int32), axis=-1
+    ).astype(jnp.int32)
+    first_block = start[:, 0] // local_len
+    upstream = out_cotangent.astype(jnp.float32).reshape(tok_count, width)
+    branch_full = valid_rows * upstream
+    branch_grad = branch_full.astype(jnp.bfloat16)
+    grad_attended = contract_cols(branch_grad, out_weight).astype(jnp.bfloat16)
+    grad_attended = (
+        grad_attended.reshape(rows, local_len, HEADS, HEAD_DIM)
+        .transpose(0, 3, 2, 1)
+        .reshape(rows, HEAD_DIM, HEADS * local_len)
+    )
+    attended, grad_query, keyval_terms = attention(
+        first_block,
+        lax.axis_index("seq").astype(jnp.int32)[None],
+        queries,
+        grad_attended,
+        keyval_all,
+        start[:, None, :],
+        cos_table.T,
+        sin_table.T,
+    )
+    attended_flat = attended.transpose(0, 2, 1).reshape(tok_count, width)
+    grad_query_pre = grad_query.transpose(0, 2, 1).reshape(tok_count, width)
+    attn_out = jnp.dot(attended_flat, out_weight, preferred_element_type=jnp.float32) + out_bias
+    dense_full, dense_pull = jax.vjp(layer_norm, inputs, dense_gain, dense_shift)
+    dense_in = dense_full.astype(jnp.bfloat16)
+    hidden = jnp.dot(dense_in, up_weight, preferred_element_type=jnp.float32) + up_bias
+    activated_full, gelu_pull = jax.vjp(partial(jax.nn.gelu, approximate=False), hidden)
+    activated = activated_full.astype(jnp.bfloat16)
+    dense_out = jnp.dot(activated, down_weight, preferred_element_type=jnp.float32) + down_bias
+    layer_out = (
+        (inputs + valid_rows * (attn_out + dense_out))
+        .astype(jnp.bfloat16)
+        .reshape(rows, local_len, width)
+    )
+    branch_sum = jnp.sum(branch_full, axis=0)
+    grad_out_weight = contract_rows(attended_flat, branch_grad)
+    grad_down_weight = contract_rows(activated, branch_grad)
+    (grad_hidden_full,) = gelu_pull(contract_cols(branch_grad, down_weight))
+    grad_hidden = grad_hidden_full.astype(jnp.bfloat16)
+    grad_up_weight = contract_rows(dense_in, grad_hidden)
+    grad_up_bias = jnp.sum(grad_hidden.astype(jnp.float32), axis=0)
+    grad_dense_in = contract_cols(grad_hidden, up_weight)
+    dense_back, grad_dense_gain, grad_dense_shift = dense_pull(grad_dense_in)
+    keyval_grad = lax.psum_scatter(
+        keyval_terms.reshape(rows, full_len, 2 * HEAD_DIM),
+        "seq",
+        scatter_dimension=1,
+        tiled=True,
+    ).astype(jnp.float32) + keyval_cotangent.astype(jnp.float32)
+    grad_key_pre = unrotate(keyval_grad[..., :HEAD_DIM], cos_table, sin_table)
+    grad_keyval_pre = (
+        jnp.concatenate([grad_key_pre, keyval_grad[..., HEAD_DIM:]], axis=-1)
+        .reshape(tok_count, 2 * HEAD_DIM)
+        .astype(jnp.bfloat16)
+    )
+    grad_query_weight = contract_rows(normed, grad_query_pre)
+    grad_query_bias = jnp.sum(grad_query_pre.astype(jnp.float32), axis=0)
+    grad_keyval_weight = contract_rows(normed, grad_keyval_pre)
+    grad_keyval_bias = jnp.sum(grad_keyval_pre.astype(jnp.float32), axis=0)
+    grad_normed = contract_cols(grad_query_pre, query_weight) + contract_cols(
+        grad_keyval_pre, keyval_weight
+    )
+    attention_back, grad_attention_gain, grad_attention_shift = attention_pull(grad_normed)
+    grad_tokens = (
+        (upstream + attention_back + dense_back)
+        .astype(jnp.bfloat16)
+        .reshape(rows, local_len, width)
+    )
+    local_grads = (
+        grad_query_weight,
+        grad_query_bias,
+        grad_keyval_weight,
+        grad_keyval_bias,
+        grad_out_weight,
+        branch_sum,
+        grad_up_weight,
+        grad_up_bias,
+        grad_down_weight,
+        branch_sum,
+        grad_attention_gain,
+        grad_attention_shift,
+        grad_dense_gain,
+        grad_dense_shift,
+    )
+    shares = (
+        lax.psum_scatter(
+            local_grads[0].astype(jnp.bfloat16), "seq", scatter_dimension=0, tiled=True
+        ).astype(jnp.float32),
+        lax.psum_scatter(
+            local_grads[1].astype(jnp.bfloat16), "seq", scatter_dimension=0, tiled=True
+        ).astype(jnp.float32),
+        lax.psum_scatter(
+            local_grads[2].astype(jnp.bfloat16), "seq", scatter_dimension=0, tiled=True
+        ).astype(jnp.float32),
+        lax.psum_scatter(
+            local_grads[3].astype(jnp.bfloat16), "seq", scatter_dimension=0, tiled=True
+        ).astype(jnp.float32),
+        lax.psum_scatter(
+            local_grads[4].astype(jnp.bfloat16), "seq", scatter_dimension=0, tiled=True
+        ).astype(jnp.float32),
+        lax.psum_scatter(
+            local_grads[5].astype(jnp.bfloat16), "seq", scatter_dimension=0, tiled=True
+        ).astype(jnp.float32),
+        lax.psum_scatter(
+            local_grads[6].astype(jnp.bfloat16), "seq", scatter_dimension=0, tiled=True
+        ).astype(jnp.float32),
+        lax.psum_scatter(
+            local_grads[7].astype(jnp.bfloat16), "seq", scatter_dimension=0, tiled=True
+        ).astype(jnp.float32),
+        lax.psum_scatter(
+            local_grads[8].astype(jnp.bfloat16), "seq", scatter_dimension=0, tiled=True
+        ).astype(jnp.float32),
+        lax.psum_scatter(
+            local_grads[9].astype(jnp.bfloat16), "seq", scatter_dimension=0, tiled=True
+        ).astype(jnp.float32),
+        lax.psum_scatter(
+            local_grads[10].astype(jnp.bfloat16), "seq", scatter_dimension=0, tiled=True
+        ).astype(jnp.float32),
+        lax.psum_scatter(
+            local_grads[11].astype(jnp.bfloat16), "seq", scatter_dimension=0, tiled=True
+        ).astype(jnp.float32),
+        lax.psum_scatter(
+            local_grads[12].astype(jnp.bfloat16), "seq", scatter_dimension=0, tiled=True
+        ).astype(jnp.float32),
+        lax.psum_scatter(
+            local_grads[13].astype(jnp.bfloat16), "seq", scatter_dimension=0, tiled=True
+        ).astype(jnp.float32),
+    )
+    totals = (
+        lax.psum(shares[0].astype(jnp.bfloat16), "batch").astype(jnp.float32),
+        lax.psum(shares[1].astype(jnp.bfloat16), "batch").astype(jnp.float32),
+        lax.psum(shares[2].astype(jnp.bfloat16), "batch").astype(jnp.float32),
+        lax.psum(shares[3].astype(jnp.bfloat16), "batch").astype(jnp.float32),
+        lax.psum(shares[4].astype(jnp.bfloat16), "batch").astype(jnp.float32),
+        lax.psum(shares[5].astype(jnp.bfloat16), "batch").astype(jnp.float32),
+        lax.psum(shares[6].astype(jnp.bfloat16), "batch").astype(jnp.float32),
+        lax.psum(shares[7].astype(jnp.bfloat16), "batch").astype(jnp.float32),
+        lax.psum(shares[8].astype(jnp.bfloat16), "batch").astype(jnp.float32),
+        lax.psum(shares[9].astype(jnp.bfloat16), "batch").astype(jnp.float32),
+        lax.psum(shares[10].astype(jnp.bfloat16), "batch").astype(jnp.float32),
+        lax.psum(shares[11].astype(jnp.bfloat16), "batch").astype(jnp.float32),
+        lax.psum(shares[12].astype(jnp.bfloat16), "batch").astype(jnp.float32),
+        lax.psum(shares[13].astype(jnp.bfloat16), "batch").astype(jnp.float32),
+    )
+    return (
+        layer_out,
+        keyval_local,
+        grad_tokens,
+        totals[0],
+        totals[1],
+        totals[2],
+        totals[3],
+        totals[4],
+        totals[5],
+        totals[6],
+        totals[7],
+        totals[8],
+        totals[9],
+        totals[10],
+        totals[11],
+        totals[12],
+        totals[13],
+    )
+
+
+def choose(tokens, *rest):
+    return (local if tokens.shape[1] % 128 == 0 else local_plain)(tokens, *rest)
+
+
 def solution(mesh):
     placed = (
         P("batch", "seq", None),
@@ -349,7 +712,7 @@
         P("batch", "seq", None),
     )
     return jax.shard_map(
-        local,
+        choose,
         mesh=mesh,
         in_specs=placed,
         out_specs=(

time: 1880 us -> 736 us (0.39)
  matrix products: 860 us -> 206 us
  local copies, waits for them, and re-layouts: 411 us -> 63.1 us
  other arithmetic: 298 us -> 45.4 us
  waiting for transfers between devices: 199 us -> 283 us
  Pallas kernels: 0 us -> 36.3 us
    dot_general x29 -> x5, matrix products: 411 us -> 71.4 us  [contract_cols(): lax.dot_general(left_side, right_side, (((1,), (1,)), ((), ())), preferre...]
    broadcast_in_dim x32 -> x1, local copies, waits for them, and re-layouts: 230 us -> 0.61 us  [local(): start[:, None, :]]
    dot_general x16 -> x0, matrix products: 181 us -> none  [the longest x8 118 us: forward_row(): jnp.dot(weights, keyval_row[:, HEAD_DIM:], preferred_element_type=jnp.flo...]
    convert_element_type x9 -> x0, other arithmetic: 139 us -> none  [the longest x8 136 us: backward_row(): grad_scores = (probs * (grad_probs - inner)).astype(jnp.bfloat16)]
    dot_general x21 -> x5, matrix products: 178 us -> 43.3 us  [contract_rows(): lax.dot_general(left_side, right_side, (((0,), (0,)), ((), ())), preferre...]
    reduce_scatter x1, waiting for transfers between devices: 43.2 us -> 137 us  [local(): lax.psum_scatter(local_grads[0].astype(jnp.bfloat16), 'seq', scatter_dime...]
    reduce_sum x8 -> x1, other arithmetic: 92.9 us -> 1.81 us  [local(): jnp.sum((order_all[:, None, :] < order_own[:, :, None]).astype(jnp.int32)...]
    pallas_call x0 -> x1, Pallas kernels: none -> 36.3 us  [attention(): pl.pallas_call(partial(attn_kernel, blk=blk, nblk=nblk), out_shape=[jax.S...]
  transfers between devices with their start and end apart: 8 -> 8, of which waited for: 4 -> 5; matrix products, arithmetic and copies ran while one was open for 80% -> 39% of each run, Pallas kernels for 0% -> 5%
where the time goes in v1:
time: 736 us; the launch traced here: 732 us
  waiting for transfers between devices  283 us (38%)
  matrix products  206 us (28%)
  blocking collectives  79.7 us (11%)
  local copies, waits for them, and re-layouts  63.1 us (9%)
  other arithmetic  45.4 us (6%)
  Pallas kernels  36.3 us (5%)
  between operations  17.2 us (2%)
    reduce_scatter x1, waiting for transfers between devices, local(): lax.psum_scatter(local_grads[0].astype(jnp.bfloat16), 'seq', scatter_dime...  137 us
    dot_general x5, matrix products, contract_cols(): lax.dot_general(left_side, right_side, (((1,), (1,)), ((), ())), preferre...  71.4 us
    reduce_scatter x1, waiting for transfers between devices, local(): lax.psum_scatter(keyval_terms.reshape(rows, full_len, 2 * HEAD_DIM), 'seq...  67.3 us
    reduce_scatter x1, waiting for transfers between devices, local(): lax.psum_scatter(local_grads[4].astype(jnp.bfloat16), 'seq', scatter_dime...  66.9 us
    dot_general x1, matrix products, local(): jnp.dot(dense_in, up_weight, preferred_element_type=jnp.float32) + up_bias  64.6 us
    dot_general x5, matrix products, contract_rows(): lax.dot_general(left_side, right_side, (((0,), (0,)), ((), ())), preferre...  43.3 us
    pallas_call x1, Pallas kernels, attention(): pl.pallas_call(partial(attn_kernel, blk=blk, nblk=nblk), out_shape=[jax.S...  36.3 us
    unnamed x1, blocking collectives  35.9 us
  transfers between devices with their start and end apart: 8, of which 5 were waited for; matrix products, arithmetic and copies ran while one was open for 39% of the time, Pallas kernels for 5%

profile of v1, /device:TPU:0, one launch (start us, length us, event | category | flops | bytes accessed | tf_op | source)
XLA Modules:
  0.0 732.2 jit_solution(3694513455338913648)
XLA Ops:
  23.5 64.6 %multiply_convert_fusion = (bf16[2048,3072]{1,0:T(8,128)(2,1)S(1)}, f32[2048,3072]{1,0:T(8,128)}, f32[2048,3072]{1,0:T(8,128)}) fusion(f32[3072]{0:T(1024)S(1)} %copy-done.48, bf16[2048,768]{1,0:T(8,128)(2,1)} %get-tuple-element.60, bf16[768,3072]{1,0:T(8,128)(2,1)} %param.26), kind=kOutput, calls=%fused_computation.3 | convolution fusion | flops 10078912512 | bytes 70791168 | tf_op jit(solution)/shard_map/dot_general | solution.py:549
  93.6 12.3 %convolution_convert_fusion = bf16[3072,768]{1,0:T(8,128)(2,1)} fusion(bf16[2048,3072]{1,0:T(8,128)(2,1)S(1)} %get-tuple-element.56, bf16[2048,768]{1,0:T(8,128)(2,1)S(1)} %fusion.8), kind=kOutput, calls=%fused_computation.56 | convolution fusion | flops 9666035712 | bytes 20447232 | tf_op jit(solution)/shard_map/dot_general | solution.py:65
  106.4 33.5 %fusion.62 = (bf16[3072]{0:T(1024)(128)(2,1)S(1)}, bf16[2048,3072]{1,0:T(8,128)(2,1)}) fusion(f32[2048,3072]{1,0:T(8,128)} %get-tuple-element.57, bf16[2048,768]{1,0:T(8,128)(2,1)} %copy-done.9, bf16[3072,768]{1,0:T(8,128)(2,1)} %param.28, f32[2048,3072]{1,0:T(8,128)} %get-tuple-element.80, f32[3072]{0:T(1024)S(1)} %copy-done.48), kind=kOutput, calls=%fused_computation.115 | convolution fusion | flops 9764336640 | bytes 70797312 | tf_op jit(solution)/shard_map/dot_general | solution.py:71
  140.0 15.5 %convolution_convert_fusion.1 = bf16[768,3072]{1,0:T(8,128)(2,1)} fusion(bf16[2048,768]{1,0:T(8,128)(2,1)} %get-tuple-element.60, bf16[2048,3072]{1,0:T(8,128)(2,1)} %get-tuple-element.83), kind=kOutput, calls=%fused_computation.57 | convolution fusion | flops 9666035712 | bytes 20447232 | tf_op jit(solution)/shard_map/dot_general | solution.py:65
  155.5 32.9 %all_gather.6 = s32[8,2048]{1,0:T(8,128)S(1)} all-gather(s32[8,256]{1,0:T(8,128)S(1)} %copy-done.27), channel_id=1, replica_groups=mesh['batch'=4,'seq'=8] {'seq'}, dimensions={1}, use_global_device_ids=true | all-gather | bytes 73728 | tf_op jit(solution)/shard_map/all_gather | solution.py:516
  190.9 6.2 convolution_convert_fusion.2
  197.1 4.9 copy.87
  205.0 3.9 copy.88
  208.9 6.8 reshape.329.do_ref
  215.7 7.2 convolution_add_fusion.1
  222.8 6.6 copy.85
  229.4 5.9 copy.104
  236.6 3.9 copy.86
  240.5 6.8 reshape.326.q_ref
  248.6 36.3 %attention.1 = (bf16[8,768,256]{2,1,0:T(8,128)(2,1)}, bf16[8,768,256]{2,1,0:T(8,128)(2,1)}, bf16[8,8,256,128]{3,2,1,0:T(8,128)(2,1)}) custom-call(s32[8]{0:T(128)} %and_select_fusion.first_ref, s32[1]{0:T(128)} %bitcast.1.sidx_ref, bf16[8,64,3072]{2,1,0:T(8,128)(2,1)} %reshape.326.q_ref, bf16[8,64,3072]{2,1,0:T(8,128)(2,1)} %reshape.329.do_ref, ...), custom_call_target="tpu_custom_call" | custom-call | tf_op jit(solution)/shard_map/attention/pallas_call | solution.py:201
  285.0 6.2 bitcast_convert_fusion.1
  291.2 6.6 bitcast_convert_fusion
  298.0 5.3 reduce-scatter.15.cloned.1.call-done
  303.3 136.9 %reduce-scatter.9.cloned.1.call-done = bf16[96,768]{1,0:T(8,128)(2,1)} async-done(((bf16[768,768]{1,0:T(8,128)(2,1)}), bf16[96,768]{1,0:T(8,128)(2,1)}) %reduce-scatter.9.cloned.1.call-update) | async-done | bytes 147472 | tf_op jit(solution)/shard_map/reduce_scatter | solution.py:609
  440.2 66.9 %reduce-scatter.13.cloned.1.call-done = bf16[96,768]{1,0:T(8,128)(2,1)} async-done(((bf16[768,768]{1,0:T(8,128)(2,1)}), bf16[96,768]{1,0:T(8,128)(2,1)}) %reduce-scatter.13.cloned.1.call-update) | async-done | bytes 147472 | tf_op jit(solution)/shard_map/reduce_scatter | solution.py:621
  513.4 16.1 %fusion.65 = f32[2048,768]{1,0:T(8,128)} fusion(bf16[2048,3072]{1,0:T(8,128)(2,1)} %get-tuple-element.83, bf16[768,3072]{1,0:T(8,128)(2,1)} %param.26), kind=kOutput, calls=%fused_computation.118 | convolution fusion | flops 9663676416 | bytes 23592960 | tf_op jit(solution)/shard_map/dot_general | solution.py:71
  531.9 4.7 copy.94
  536.7 4.7 copy.93
  541.3 7.3 fusion.64
  551.4 16.1 %fusion.34 = bf16[2048,768]{1,0:T(8,128)(2,1)} fusion(bf16[8,256,768]{2,1,0:T(8,128)(2,1)S(1)} %copy-done.3, f32[2048,768]{1,0:T(8,128)S(1)} %fusion.63, bf16[2048,3072]{1,0:T(8,128)(2,1)} %copy-done.54, bf16[3072,768]{1,0:T(8,128)(2,1)} %param.28, f32[768]{0:T(1024)S(1)} %copy-done.50, f32[768]{0:T(1024)S(1)} %copy-done.51, f32[2048]{0:T(1024)S(1)} %bitcast.156), kind=kOutput, calls=%fused_computation.55 | convolution fusion | flops 9674686464 | bytes 29898752 | tf_op jit(solution)/shard_map/dot_general | solution.py:552
  575.2 67.3 %reduce-scatter.7.cloned.1.call-done = bf16[8,256,128]{2,1,0:T(8,128)(2,1)} async-done(((bf16[8,2048,128]{2,1,0:T(8,128)(2,1)}), bf16[8,256,128]{2,1,0:T(8,128)(2,1)}) %reduce-scatter.7.cloned.1.call-update) | async-done | bytes 524304 | tf_op jit(solution)/shard_map/reduce_scatter | solution.py:567
  648.6 8.2 %fusion.59 = (bf16[768]{0:T(1024)(128)(2,1)S(1)}, f32[2048]{0:T(1024)S(1)}, f32[2048]{0:T(1024)S(1)}, bf16[768]{0:T(1024)(128)(2,1)S(1)}, f32[2048,768]{1,0:T(8,128)S(1)}) fusion(f32[768]{0:T(1024)S(1)} %copy-done.33, f32[2048]{0:T(1024)S(1)} %bitcast.150, bf16[8,256,768]{2,1,0:T(8,128)(2,1)} %param.18, f32[2048,768]{1,0:T(8,128)} %fusion.65, ...), kind=kOutput, calls=%fused_computation.113 | convolution fusion | flops 419949056 | bytes 22774784 | tf_op jit(solution)/shard_map/dot_general | solution.py:71
  656.8 5.4 fusion.31
  662.3 5.2 fusion.10
  667.4 35.9 %all-reduce.8 = (bf16[768]{0:T(1024)(128)(2,1)S(1)}, bf16[128]{0:T(256)(128)(2,1)S(1)}, bf16[768]{0:T(1024)(128)(2,1)S(1)}, bf16[3072]{0:T(1024)(128)(2,1)S(1)},...) all-reduce(bf16[768]{0:T(1024)(128)(2,1)S(1)} %reduce_sum.160, ...), channel_id=4, replica_groups=mesh['batch'=4,'seq'=8] {'seq'}, use_global_device_ids=true, to_apply=%region_11.12.clone | all-reduce | flops 7808 | bytes 31232
  704.0 5.6 reduce-scatter.11.cloned.1.call-done
  709.5 10.8 %all-reduce.9 = (bf16[96]{0:T(256)(128)(2,1)S(1)}, bf16[96,128]{1,0:T(8,128)(2,1)S(1)}, bf16[16]{0:T(256)(128)(2,1)S(1)}, bf16[96]{0:T(256)(128)(2,1)S(1)}, bf16...) all-reduce(bf16[96]{0:T(256)(128)(2,1)S(1)} %dynamic-slice.1, ...), channel_id=1, replica_groups=mesh['batch'=4,'seq'=8] {'batch'}, use_global_device_ids=true, to_apply=%region_12.13 | all-reduce | flops 13264 | bytes 53056 | tf_op jit(solution)/shard_map/psum | solution.py:654
  (202 shorter events, 58.5 us)
Async XLA Ops:
  7.2 208.5 %copy-start = (bf16[768,768]{1,0:T(8,128)(2,1)S(1)}, bf16[768,768]{1,0:T(8,128)(2,1)}, u32[]{:S(2)}) copy-start(bf16[768,768]{1,0:T(8,128)(2,1)} %param.20) | copy-start | bytes 3538948
  7.2 241.4 %all-gather.2.cloned.1.call-start = ((), (), s32[]{:S(2)}) async-start(), calls=%async_computation.6 | async-start | bytes 4718592 | tf_op jit(solution)/shard_map/all_gather | solution.py:515
  7.3 12.2 %copy-start.44 = (f32[8]{0:T(128)}, f32[8]{0:T(128)S(1)}, u32[]{:S(2)}) copy-start(f32[8]{0:T(128)S(1)} %multiply_power_fusion) | copy-start | bytes 100
  9.9 8.3 %copy-start.16 = (bf16[768,128]{1,0:T(8,128)(2,1)S(1)}, bf16[768,128]{1,0:T(8,128)(2,1)}, u32[]{:S(2)}) copy-start(bf16[768,128]{1,0:T(8,128)(2,1)} %param.22) | copy-start | bytes 589828
  9.9 8.3 %copy-start.46 = (f32[128]{0:T(128)S(1)}, f32[128]{0:T(128)}, u32[]{:S(2)}) copy-start(f32[128]{0:T(128)} %param.23) | copy-start | bytes 1540
  19.9 68.3 %copy-start.12 = (f32[256,8]{1,0:T(8,128)}, f32[256,8]{1,0:T(8,128)S(1)}, u32[]{:S(2)}) copy-start(f32[256,8]{1,0:T(8,128)S(1)} %copy.90) | copy-start | bytes 24580
  20.5 67.7 %copy-start.14 = (f32[256,8]{1,0:T(8,128)}, f32[256,8]{1,0:T(8,128)S(1)}, u32[]{:S(2)}) copy-start(f32[256,8]{1,0:T(8,128)S(1)} %copy.91) | copy-start | bytes 24580
  23.2 274.8 %reduce-scatter.17.cloned.1.call-start = ((), (), s32[]{:S(2)}) async-start(), calls=%async_computation.12 | async-start | bytes 5308416 | tf_op jit(solution)/shard_map/reduce_scatter | solution.py:633
  23.5 64.7 %copy-start.27 = (s32[8,256]{1,0:T(8,128)S(1)}, s32[8,256]{1,0:T(8,128)}, u32[]{:S(2)}) copy-start(s32[8,256]{1,0:T(8,128)} %param.19) | copy-start | bytes 24580
  23.5 64.7 %copy-start.6 = (bf16[8,256,768]{2,1,0:T(8,128)(2,1)S(1)}, bf16[8,256,768]{2,1,0:T(8,128)(2,1)}, u32[]{:S(2)}) copy-start(bf16[8,256,768]{2,1,0:T(8,128)(2,1)} %param.34) | copy-start | bytes 9437188
  105.9 197.3 %reduce-scatter.15.cloned.1.call-start = ((), (), s32[]{:S(2)}) async-start(), calls=%async_computation.11 | async-start | bytes 5308416 | tf_op jit(solution)/shard_map/reduce_scatter | solution.py:627
  140.0 50.9 %copy-start.47 = (bf16[768,768]{1,0:T(8,128)(2,1)S(1)}, bf16[768,768]{1,0:T(8,128)(2,1)}, u32[]{:S(2)}) copy-start(bf16[768,768]{1,0:T(8,128)(2,1)} %param.24) | copy-start | bytes 3538948
  155.5 284.7 %reduce-scatter.9.cloned.1.call-start = ((), (), s32[]{:S(2)}) async-start(), calls=%async_computation.8 | async-start | bytes 1327104 | tf_op jit(solution)/shard_map/reduce_scatter | solution.py:609
  205.0 10.7 %copy-start.49 = (f32[768]{0:T(1024)S(1)}, f32[768]{0:T(1024)}, u32[]{:S(2)}) copy-start(f32[768]{0:T(1024)} %param.21) | copy-start | bytes 9220
  236.5 11.4 %copy-start.43 = (f32[256]{0:T(256)S(1)}, f32[256]{0:T(256)}, u32[]{:S(2)}) copy-start(f32[256]{0:T(256)} %copy-done.42) | copy-start | bytes 3076
  236.5 11.4 %copy-start.45 = (f32[8]{0:T(128)S(1)}, f32[8]{0:T(128)}, u32[]{:S(2)}) copy-start(f32[8]{0:T(128)} %copy-done.44) | copy-start | bytes 100
  247.3 37.7 %copy-start.33 = (f32[768]{0:T(1024)S(1)}, f32[768]{0:T(1024)}, u32[]{:S(2)}) copy-start(f32[768]{0:T(1024)} %param.30) | copy-start | bytes 9220
  247.3 37.7 %copy-start.35 = (f32[8,256]{1,0:T(8,128)S(1)}, f32[8,256]{1,0:T(8,128)}, u32[]{:S(2)}) copy-start(f32[8,256]{1,0:T(8,128)} %copy-done.34) | copy-start | bytes 24580
  247.3 37.7 %copy-start.38 = (f32[8,256]{1,0:T(8,128)S(1)}, f32[8,256]{1,0:T(8,128)}, u32[]{:S(2)}) copy-start(f32[8,256]{1,0:T(8,128)} %get-tuple-element.70) | copy-start | bytes 24580
  247.3 37.7 %copy-start.41 = (f32[768]{0:T(1024)S(1)}, f32[768]{0:T(1024)}, u32[]{:S(2)}) copy-start(f32[768]{0:T(1024)} %param.31) | copy-start | bytes 9220
  248.6 36.3 %copy-start.2 = (bf16[8,256,768]{2,1,0:T(8,128)(2,1)S(1)}, bf16[8,256,768]{2,1,0:T(8,128)(2,1)}, u32[]{:S(2)}) copy-start(bf16[8,256,768]{2,1,0:T(8,128)(2,1)} %param.18) | copy-start | bytes 9437188
  291.2 215.9 %reduce-scatter.13.cloned.1.call-start = ((), (), s32[]{:S(2)}) async-start(), calls=%async_computation.10 | async-start | bytes 1327104 | tf_op jit(solution)/shard_map/reduce_scatter | solution.py:621
  297.9 210.4 %copy-start.52 = (u32[32]{0:T(128)S(1)}, u32[32]{0:T(128)}, u32[]{:S(2)}) copy-start(u32[32]{0:T(128)} %constant.115) | copy-start | bytes 388
  297.9 269.6 %all-reduce.13.cloned.1.call-start = ((), (), s32[]{:S(2)}) async-start(), calls=%async_computation.13 | async-start | bytes 2949120 | tf_op jit(solution)/shard_map/psum | solution.py:653
  507.1 135.4 %reduce-scatter.7.cloned.1.call-start = ((), (), s32[]{:S(2)}) async-start(), calls=%async_computation.7 | async-start | bytes 4718592 | tf_op jit(solution)/shard_map/reduce_scatter | solution.py:567
  507.9 201.7 %reduce-scatter.11.cloned.1.call-start = ((), (), s32[]{:S(2)}) async-start(), calls=%async_computation.9 | async-start | bytes 221184 | tf_op jit(solution)/shard_map/reduce_scatter | solution.py:615
  551.4 91.1 %copy-start.18 = (bf16[8,256,128]{2,1,0:T(8,128)(2,1)S(1)}, bf16[8,256,128]{2,1,0:T(8,128)(2,1)}, u32[]{:S(2)}) copy-start(bf16[8,256,128]{2,1,0:T(8,128)(2,1)} %param.35) | copy-start | bytes 1572868
  567.5 76.5 %copy-start.13 = (f32[256,8]{1,0:T(8,128)S(1)}, f32[256,8]{1,0:T(8,128)}, u32[]{:S(2)}) copy-start(f32[256,8]{1,0:T(8,128)} %copy-done.12) | copy-start | bytes 24580
  567.5 76.5 %copy-start.15 = (f32[256,8]{1,0:T(8,128)S(1)}, f32[256,8]{1,0:T(8,128)}, u32[]{:S(2)}) copy-start(f32[256,8]{1,0:T(8,128)} %copy-done.14) | copy-start | bytes 24580
  645.8 11.0 %slice-start = ((s8[6291456]{0:T(1024)(128)(4,1)}), s8[2097152]{0:T(1024)(128)(4,1)S(1)}, s32[]{:S(2)}) async-start(s8[6291456]{0:T(1024)(128)(4,1)} %bitcast.132), calls=%async_computation.14 | async-start | bytes 4194304
  648.5 8.3 %copy-start.5 = (bf16[8,256,768]{2,1,0:T(8,128)(2,1)S(1)}, bf16[8,256,768]{2,1,0:T(8,128)(2,1)}, u32[]{:S(2)}) copy-start(bf16[8,256,768]{2,1,0:T(8,128)(2,1)} %param.18) | copy-start | bytes 9437188
  648.5 8.3 %slice-start.1 = ((s8[6291456]{0:T(1024)(128)(4,1)}), s8[4194304]{0:T(1024)(128)(4,1)S(1)}, s32[]{:S(2)}) async-start(s8[6291456]{0:T(1024)(128)(4,1)} %bitcast.132), calls=%async_computation.15 | async-start | bytes 8388608
  (33 other events, 140.6 us)
Sparse Core Ops, SparseCore 0:
  23.4 76.0 all-gather.1
  106.0 98.2 reduce-scatter.16
  208.0 95.1 reduce-scatter.14
  307.1 133.0 reduce-scatter.8
  444.0 63.0 reduce-scatter.12
  509.5 40.7 all-reduce.12
  554.4 87.9 reduce-scatter.6
  648.6 60.8 reduce-scatter.10

commit v2 on v0

--- a/solution.py
+++ b/solution.py
@@ -3,11 +3,16 @@
 import jax
 import jax.numpy as jnp
 from jax import lax
+from jax.experimental import pallas as pl
+from jax.experimental.pallas import tpu as pltpu
 from jax.sharding import PartitionSpec as P
 
 HEADS = 12
 HEAD_DIM = 64
 ROT = 16
+LOG2E = 1.4426950408889634
+f32 = jnp.float32
+bf16 = jnp.bfloat16
 
 
 epsilon = 1e-05
@@ -69,7 +74,7 @@
     )
 
 
-def local(
+def local_plain(
     tokens,
     segment_ids,
     query_weight,
@@ -327,6 +332,1005 @@
     )
 
 
+ROT_HALF = ROT // 2
+
+
+def nn(left, right):
+    return lax.dot_general(left, right, (((1,), (0,)), ((), ())), preferred_element_type=f32)
+
+
+def nt(left, right):
+    return lax.dot_general(left, right, (((1,), (1,)), ((), ())), preferred_element_type=f32)
+
+
+def tn(left, right):
+    return lax.dot_general(left, right, (((0,), (0,)), ((), ())), preferred_element_type=f32)
+
+
+def tt(left, right):
+    return lax.dot_general(left, right, (((0,), (1,)), ((), ())), preferred_element_type=f32)
+
+
+def standardize(values):
+    centred = values - jnp.mean(values, axis=-1, keepdims=True)
+    variance = jnp.mean(centred * centred, axis=-1, keepdims=True)
+    spread = lax.rsqrt(variance + epsilon)
+    return centred * spread, spread
+
+
+def turn(columns, cos, sin):
+    a, b = columns[0:ROT_HALF], columns[ROT_HALF:ROT]
+    return jnp.concatenate([a * cos - b * sin, b * cos + a * sin, columns[ROT:]], axis=0)
+
+
+def turn_back(columns, cos, sin):
+    a, b = columns[0:ROT_HALF], columns[ROT_HALF:ROT]
+    return jnp.concatenate([a * cos + b * sin, b * cos - a * sin, columns[ROT:]], axis=0)
+
+
+def params(megabytes, **rest):
+    return pltpu.CompilerParams(vmem_limit_bytes=megabytes * 2**20, **rest)
+
+
+def cost(flops, moved):
+    return pl.CostEstimate(flops=int(flops), bytes_accessed=int(moved), transcendentals=0)
+
+
+def whole(*shape):
+    return pl.BlockSpec(shape, lambda *_: (0,) * len(shape))
+
+
+def norm_kernel(
+    live_ref, x_ref, cot_ref, seg_ref, ag_ref, as_ref, dg_ref, ds_ref, kw_ref, kb_ref, cos_ref, sin_ref,
+    normed_ref, dense_ref, kv_ref, bg_ref,
+):
+    position = lax.broadcasted_iota(jnp.int32, (x_ref.shape[0], 1), 0)
+    alive = position < live_ref[pl.program_id(0)]
+    bg_ref[...] = jnp.where(alive, cot_ref[...].astype(f32), 0.0).astype(bf16)
+    unit, _ = standardize(x_ref[...].astype(f32))
+    normed = (unit * ag_ref[...] + as_ref[...]).astype(bf16)
+    normed_ref[...] = normed
+    dense_ref[...] = (unit * dg_ref[...] + ds_ref[...]).astype(bf16)
+    keyval = (nn(normed, kw_ref[...]) + kb_ref[...]).T
+    blk = keyval.shape[1]
+    keyval = turn(keyval, cos_ref[...], sin_ref[...])
+    kv_ref[0, 0:blk, :] = keyval.T.astype(bf16)
+    ids = seg_ref[0].astype(f32)
+    kv_ref[0, blk:, :] = jnp.concatenate(
+        [ids, jnp.zeros((16 - ids.shape[0], 128), f32)], axis=0
+    ).astype(bf16)
+
+
+def norms(live, x, cot, seg, again, ashift, dgain, dshift, kw, kb, cos, sin, rows, blk):
+    tok, width = x.shape
+    tile = pl.BlockSpec((blk, width), lambda r, *_: (r, 0))
+    return pl.pallas_call(
+        norm_kernel,
+        grid_spec=pltpu.PrefetchScalarGridSpec(
+            num_scalar_prefetch=1,
+            grid=(rows,),
+            in_specs=[
+                tile, tile,
+                pl.BlockSpec((1, blk // 128, 128), lambda r, *_: (r, 0, 0)),
+                whole(1, width), whole(1, width), whole(1, width), whole(1, width),
+                whole(width, 2 * HEAD_DIM), whole(1, 2 * HEAD_DIM),
+                whole(ROT_HALF, blk), whole(ROT_HALF, blk),
+            ],
+            out_specs=[
+                tile, tile, pl.BlockSpec((1, blk + 16, 2 * HEAD_DIM), lambda r, *_: (r, 0, 0)), tile,
+            ],
+        ),
+        out_shape=[
+            jax.ShapeDtypeStruct((tok, width), bf16),
+            jax.ShapeDtypeStruct((tok, width), bf16),
+            jax.ShapeDtypeStruct((rows, blk + 16, 2 * HEAD_DIM), bf16),
+            jax.ShapeDtypeStruct((tok, width), bf16),
+        ],
+        compiler_params=params(32),
+        cost_estimate=cost(2 * tok * width * 2 * HEAD_DIM, 10 * tok * width),
+        name="norms",
+    )(live, x, cot, seg, again, ashift, dgain, dshift, kw, kb, cos, sin)
+
+
+def heads_kernel(
+    normed_ref, bg_ref, qw_ref, qb_ref, ow_ref, cos_ref, sin_ref,
+    q_ref, do_ref,
+):
+    blk = normed_ref.shape[0]
+    queries = (nn(normed_ref[...], qw_ref[...]) + qb_ref[...]).T
+    upstream = nt(ow_ref[...], bg_ref[...])
+    cos, sin = cos_ref[...], sin_ref[...]
+    for h in range(HEADS):
+        rows = slice(h * HEAD_DIM, (h + 1) * HEAD_DIM)
+        lanes = slice(h * blk, (h + 1) * blk)
+        q_ref[0, :, lanes] = (turn(queries[rows], cos, sin) * HEAD_DIM**-0.5).astype(bf16)
+        do_ref[0, :, lanes] = upstream[rows].astype(bf16)
+
+
+def heads(normed, bg, qw, qb, ow, cos, sin, rows, blk):
+    tok, width = normed.shape
+    tile = pl.BlockSpec((blk, width), lambda r: (r, 0))
+    stack = pl.BlockSpec((1, HEAD_DIM, HEADS * blk), lambda r: (r, 0, 0))
+    return pl.pallas_call(
+        heads_kernel,
+        grid=(rows,),
+        in_specs=[
+            tile, tile, whole(width, width), whole(1, width), whole(width, width),
+            whole(ROT_HALF, blk), whole(ROT_HALF, blk),
+        ],
+        out_specs=[stack, stack],
+        out_shape=[
+            jax.ShapeDtypeStruct((rows, HEAD_DIM, HEADS * blk), bf16),
+            jax.ShapeDtypeStruct((rows, HEAD_DIM, HEADS * blk), bf16),
+        ],
+        compiler_params=params(40),
+        cost_estimate=cost(4 * tok * width * width, 8 * tok * width),
+        name="heads",
+    )(normed, bg, qw, qb, ow, cos, sin)
+
+
+def gelu_parts(hidden):
+    size = jnp.abs(hidden)
+    t = 1.0 / (1.0 + (0.3275911 * 0.5**0.5) * size)
+    bell = jnp.exp2(hidden * hidden * (-0.5 * LOG2E))
+    tail = t * (0.127414796 + t * (-0.142248368 + t * (0.7107068705 + t * (-0.7265760135 + t * 0.5307027145))))
+    tail = tail * bell
+    share = jnp.where(hidden >= 0.0, 1.0 - tail, tail)
+    return share, bell * 0.3989422804014327
+
+
+def towards(axis, target):
+    return dict(device_id={axis: target}, device_id_type=pl.DeviceIdType.MESH)
+
+
+def send(src, dst, sems, at, axis, target):
+    return pltpu.make_async_remote_copy(
+        src_ref=src, dst_ref=dst, send_sem=sems.at[0, at], recv_sem=sems.at[1, at],
+        **towards(axis, target),
+    )
+
+
+def greet(planes):
+    seq, batch = lax.axis_index("seq"), lax.axis_index("batch")
+    barrier = pltpu.get_barrier_semaphore()
+    column = [lax.rem(seq + 2 * hop, 2 * planes) for hop in range(1, planes)]
+    for other in column + [seq + 1 - 2 * lax.rem(seq, 2)]:
+        pl.semaphore_signal(barrier, inc=1, **towards("seq", other))
+    for other in (batch + 1 - 2 * lax.rem(batch, 2), lax.rem(batch + 2, 4)):
+        pl.semaphore_signal(barrier, inc=1, **towards("batch", other))
+    pl.semaphore_wait(barrier, planes + 2)
+
+
+def dense_kernel(
+    di_ref, bg_ref, up_ref, ub_ref, down_ref, kv_ref,
+    act_ref, gh_ref, red_ref, gub_ref, kvs_ref,
+    hid0, hid1, gac0, gac1, act0, act1, gh0, gh1, acc_up, acc_dn, acc_ub,
+    cut_up, cut_dn, core_up, core_dn, half_up, half_dn, x_up, x_dn,
+    own_sem, z_sem, y_sem, core_sem, x_sem,
+    *, pairs, steps, tile, parts, owners,
+):
+    i = pl.program_id(0)
+    planes = owners // 2
+    seq, batch = lax.axis_index("seq"), lax.axis_index("batch")
+    plane, side = seq // 2, lax.rem(seq, 2)
+    x_at, core_at = batch // 2, lax.rem(batch, 2)
+    x_other, core_other = lax.rem(batch + 2, 4), batch + 1 - 2 * core_at
+    y_other = seq + 1 - 2 * side
+
+    def own_copy():
+        return pltpu.make_async_copy(kv_ref, kvs_ref.at[seq], own_sem)
+
+    def hop_copy(hop):
+        block = kv_ref if hop == 0 else kvs_ref.at[seq - 2 * hop]
+        return send(block, kvs_ref.at[seq - 2 * hop], z_sem, hop, "seq", seq + 2)
+
+    def across_copy(hop):
+        block = kv_ref if hop == 0 else kvs_ref.at[seq - 2 * hop]
+        return send(block, kvs_ref.at[seq - 2 * hop], y_sem, hop, "seq", y_other)
+
+    def spread(hop):
+        @pl.when(plane >= hop)
+        def _():
+            if hop > 0:
+                arrived(hop)
+            across_copy(hop).start()
+
+            @pl.when(plane < planes - 1)
+            def _():
+                hop_copy(hop).start()
+
+    def arrived(hop):
+        block = kvs_ref.at[seq - 2 * hop]
+        send(block, block, z_sem, hop - 1, "seq", y_other).wait_recv()
+
+    def settle(hop):
+        @pl.when(plane >= hop)
+        def _():
+            across_copy(hop).wait_send()
+            block = kvs_ref.at[y_other - 2 * hop]
+            send(block, block, y_sem, hop, "seq", y_other).wait_recv()
+
+            @pl.when(plane < planes - 1)
+            def _():
+                hop_copy(hop).wait_send()
+
+    def core_copies(c):
+        return [
+            send(cut_up.at[1 - core_at], core_up.at[c], core_sem, 2 * c, "batch", core_other),
+            send(cut_dn.at[1 - core_at], core_dn.at[c], core_sem, 2 * c + 1, "batch", core_other),
+        ]
+
+    def x_copies(c):
+        return [
+            send(half_up.at[1 - x_at], x_up.at[c], x_sem, 2 * c, "batch", x_other),
+            send(half_dn.at[1 - x_at], x_dn.at[c], x_sem, 2 * c + 1, "batch", x_other),
+        ]
+
+    def plus(first, second):
+        return (first.astype(f32) + second.astype(f32)).astype(bf16)
+
+    def cut(c):
+        rows, cols = cut_up.shape[3], cut_up.shape[4]
+        for core in range(2):
+            for x in range(2):
+                for o in range(owners):
+                    at = (2 * o + core) * rows
+                    cut_up[core, x, o] = acc_up[at : at + rows, x * cols : (x + 1) * cols].astype(bf16)
+                tall = cut_dn.shape[3]
+                for o in range(cut_dn.shape[2]):
+                    at = (2 * o + core) * tall
+                    cut_dn[core, x, o] = acc_dn[at : at + tall, x * cols : (x + 1) * cols].astype(bf16)
+        for copy in core_copies(c):
+            copy.start()
+
+    def halve(c):
+        for copy in core_copies(c):
+            copy.wait()
+        for x in range(2):
+            half_up[x] = plus(cut_up[core_at, x], core_up[c, x])
+            half_dn[x] = plus(cut_dn[core_at, x], core_dn[c, x])
+        for copy in x_copies(c):
+            copy.start()
+
+    def fold(c):
+        for copy in x_copies(c):
+            copy.wait()
+        rows = cut_up.shape[3]
+        few = cut_dn.shape[2]
+        red_ref[:, c * rows : (c + 1) * rows, :] = plus(half_up[x_at], x_up[c])
+        red_ref[c * few : (c + 1) * few, parts * rows :, :] = plus(half_dn[x_at], x_dn[c])
+
+    def rows_of(step, odd):
+        return pl.ds(pl.multiple_of((lax.rem(step, pairs) * 2 + odd) * tile, tile), tile)
+
+    def enter(odd, hid, gac):
+        rows = rows_of(i, odd)
+        hid[...] = nn(di_ref[rows, :], up_ref[...]) + ub_ref[...]
+        gac[...] = nt(bg_ref[rows, :], down_ref[...])
+
+    def bend(odd, hid, gac, act_s, gh_s):
+        hidden = hid[...]
+        share, bell = gelu_parts(hidden)
+        act = (hidden * share).astype(bf16)
+        grad = (gac[...] * (share + hidden * bell)).astype(bf16)
+        act_s[...] = act
+        gh_s[...] = grad
+        at = (1 - odd) * tile
+        act_ref[at : at + tile, :] = act
+        gh_ref[at : at + tile, :] = grad
+
+    def gather(odd, act_s, gh_s):
+        rows = rows_of(i - 1, odd)
+        grad = gh_s[...]
+        acc_up[...] += tn(di_ref[rows, :], grad)
+        acc_dn[...] += tn(act_s[...], bg_ref[rows, :])
+        acc_ub[...] += jnp.sum(grad.astype(f32), axis=0, keepdims=True)
+
+    def clear():
+        acc_up[...] = jnp.zeros(acc_up.shape, f32)
+        acc_dn[...] = jnp.zeros(acc_dn.shape, f32)
+        acc_ub[...] = jnp.zeros(acc_ub.shape, f32)
+
+    @pl.when(i == 0)
+    def _():
+        greet(planes)
+        own_copy().start()
+
+    @pl.when(i == 0)
+    def _():
+        clear()
+        enter(0, hid0, gac0)
+        enter(1, hid1, gac1)
+        bend(0, hid0, gac0, act0, gh0)
+
+    @pl.when((i > 0) & (i < steps))
+    def _():
+        enter(0, hid0, gac0)
+        bend(1, hid1, gac1, act1, gh1)
+        gather(0, act0, gh0)
+        enter(1, hid1, gac1)
+        bend(0, hid0, gac0, act0, gh0)
+        gather(1, act1, gh1)
+
+    @pl.when(i == steps)
+    def _():
+        bend(1, hid1, gac1, act1, gh1)
+        gather(0, act0, gh0)
+        gather(1, act1, gh1)
+
+    for c in range(parts):
+        @pl.when(i == (c + 1) * pairs)
+        def _():
+            gub_ref[c] = acc_ub[...]
+            cut(c)
+            clear()
+
+        if c < parts - 1:
+            @pl.when(i == (c + 1) * pairs + 1)
+            def _():
+                if c > 0:
+                    fold(c - 1)
+                halve(c)
+
+    for hop in range(planes):
+        @pl.when(i == hop * pairs)
+        def _():
+            spread(hop)
+
+    @pl.when(i == steps)
+    def _():
+        fold(parts - 2)
+        halve(parts - 1)
+        own_copy().wait()
+        for hop in range(planes):
+            settle(hop)
+        fold(parts - 1)
+
+
+def dense(di, bg, up, ub, down, kv, parts, owners, tile=512):
+    tok, width = di.shape
+    ff = up.shape[1]
+    chunk = ff // parts
+    pairs = tok // tile // 2
+    steps = pairs * parts
+    high, low, cols = width // owners // 2, chunk // (owners // parts) // 2, chunk // 2
+    few = owners // parts
+    at = lambda i: jnp.clip(i, 0, steps - 1)
+    anywhere = pl.BlockSpec(memory_space=pl.ANY)
+    once = lambda *shape: pl.BlockSpec(
+        shape, lambda *_: (0,) * len(shape), pipeline_mode=pl.Buffered(1)
+    )
+    dma = pltpu.SemaphoreType.DMA
+    return pl.pallas_call(
+        partial(
+            dense_kernel, pairs=pairs, steps=steps, tile=tile, parts=parts, owners=owners
+        ),
+        grid=(steps + 1,),
+        in_specs=[
+            once(tok, width),
+            once(tok, width),
+            pl.BlockSpec((width, chunk), lambda i: (0, at(i) // pairs)),
+            pl.BlockSpec((1, chunk), lambda i: (0, at(i) // pairs)),
+            pl.BlockSpec((chunk, width), lambda i: (at(i) // pairs, 0)),
+            anywhere,
+        ],
+        out_specs=[
+            pl.BlockSpec((2 * tile, chunk), lambda i: (i, 0)),
+            pl.BlockSpec((2 * tile, chunk), lambda i: (i, 0)),
+            whole(owners, parts * high + low, cols),
+            whole(parts, 1, chunk),
+            anywhere,
+        ],
+        out_shape=[
+            jax.ShapeDtypeStruct((2 * tile * (steps + 1), chunk), bf16),
+            jax.ShapeDtypeStruct((2 * tile * (steps + 1), chunk), bf16),
+            jax.ShapeDtypeStruct((owners, parts * high + low, cols), bf16),
+            jax.ShapeDtypeStruct((parts, 1, chunk), f32),
+            jax.ShapeDtypeStruct((owners,) + kv.shape, bf16),
+        ],
+        scratch_shapes=[pltpu.VMEM((tile, chunk), f32)] * 4
+        + [pltpu.VMEM((tile, chunk), bf16)] * 4
+        + [
+            pltpu.VMEM((width, chunk), f32), pltpu.VMEM((chunk, width), f32),
+            pltpu.VMEM((1, chunk), f32),
+            pltpu.VMEM((2, 2, owners, high, cols), bf16), pltpu.VMEM((2, 2, few, low, cols), bf16),
+            pltpu.VMEM((parts, 2, owners, high, cols), bf16),
+            pltpu.VMEM((parts, 2, few, low, cols), bf16),
+            pltpu.VMEM((2, owners, high, cols), bf16), pltpu.VMEM((2, few, low, cols), bf16),
+            pltpu.VMEM((parts, owners, high, cols), bf16),
+            pltpu.VMEM((parts, few, low, cols), bf16),
+            dma, dma((2, owners // 2)), dma((2, owners // 2)), dma((2, 2 * parts)),
+            dma((2, 2 * parts)),
+        ],
+        compiler_params=params(60, collective_id=0, has_side_effects=True),
+        cost_estimate=cost(8 * tok * width * ff, 8 * tok * width + 4 * tok * ff),
+        name="dense",
+    )(di, bg, up, ub, down, kv)
+
+
+def tail_kernel(
+    x_ref, cot_ref, valid_ref, att_ref, gq_ref, bg_ref, normed_ref, kcot_ref, terms_ref, gub_ref,
+    ow_ref, ob_ref, down_ref, db_ref, up_ref, qw_ref, kw_ref, ag_ref, as_ref, dg_ref, cos_ref, sin_ref,
+    *refs, rows, parts, owners,
+):
+    acts, ghs, refs = refs[:parts], refs[parts : 2 * parts], refs[2 * parts :]
+    (
+        out_ref, gt_ref, square_ref, keyval_ref, vector_ref,
+        acc, gd_s, gn_s, gk_s, vec_s,
+        own, across, below, total,
+        cut, core_in, half, x_in, piece, piece_in, part, part_in,
+        small_k, small_v, seq_k, seq_v, mid_k, mid_v, batch_k, batch_v,
+        own_sem, y_sem, z_sem, core_sem, x_sem, piece_sem, part_sem, sk_sem, sv_sem, bk_sem, bv_sem,
+    ) = refs
+    i = pl.program_id(0)
+    planes = owners // 2
+    seq, batch = lax.axis_index("seq"), lax.axis_index("batch")
+    plane, side = seq // 2, lax.rem(seq, 2)
+    x_at, core_at = batch // 2, lax.rem(batch, 2)
+    x_other, core_other = lax.rem(batch + 2, 4), batch + 1 - 2 * core_at
+    y_other = seq + 1 - 2 * side
+    high, cols = cut.shape[4], cut.shape[5]
+
+    def enter():
+        barrier = pltpu.get_barrier_semaphore()
+        for hop in range(1, owners):
+            pl.semaphore_signal(barrier, inc=1, **towards("seq", lax.rem(seq + hop, owners)))
+        for hop in range(1, parts):
+            pl.semaphore_signal(barrier, inc=1, **towards("batch", lax.rem(batch + hop, parts)))
+        pl.semaphore_wait(barrier, owners + parts - 2)
+
+    def own_copy(k):
+        return pltpu.make_async_copy(terms_ref.at[2 * k + side], own.at[k], own_sem.at[k])
+
+    def across_copy(k):
+        return send(terms_ref.at[2 * k + 1 - side], across.at[k], y_sem, k, "seq", y_other)
+
+    def below_copy(k):
+        target = lax.rem(seq + 2 * planes - 2, 2 * planes)
+        return send(own.at[k], below.at[k], z_sem, k, "seq", target)
+
+    def start_across(k):
+        @pl.when(plane >= k)
+        def _():
+            own_copy(k).start()
+            across_copy(k).start()
+
+    def tick(step):
+        k = step - (planes - 1 - plane)
+
+        @pl.when(k >= 0)
+        def _():
+            own_copy(k).wait()
+            across_copy(k).wait_recv()
+            total[...] = own[k].astype(f32) + across[k].astype(f32)
+
+            @pl.when(plane < planes - 1)
+            def _():
+                below_copy(k).wait_recv()
+                total[...] += below[k].astype(f32)
+
+            if step < planes - 1:
+                own[k] = total[...].astype(bf16)
+                below_copy(k).start()
+
+    def settle():
+        for k in range(planes):
+            @pl.when(plane >= k)
+            def _():
+                across_copy(k).wait_send()
+
+            @pl.when(plane > k)
+            def _():
+                below_copy(k).wait_send()
+
+    def core_copy():
+        return send(cut.at[1 - core_at], core_in, core_sem, 0, "batch", core_other)
+
+    def x_copy():
+        return send(half.at[1 - x_at], x_in, x_sem, 0, "batch", x_other)
+
+    def piece_copy(hop):
+        target = lax.rem(seq + hop, owners)
+        return send(piece.at[target], piece_in.at[hop - 1], piece_sem, hop - 1, "seq", target)
+
+    def part_copy(hop):
+        target = lax.rem(batch + hop, parts)
+        return send(part, part_in.at[hop - 1], part_sem, hop - 1, "batch", target)
+
+    def cut_square():
+        for m in range(2):
+            for core in range(2):
+                for x in range(2):
+                    for o in range(owners):
+                        at = (2 * o + core) * high
+                        cut[core, x, o, m] = acc[m, at : at + high, x * cols : (x + 1) * cols].astype(bf16)
+        core_copy().start()
+
+    def halve_square():
+        core_copy().wait()
+        for x in range(2):
+            half[x] = (cut[core_at, x].astype(f32) + core_in[x].astype(f32)).astype(bf16)
+        x_copy().start()
+
+    def spread_square():
+        x_copy().wait()
+        piece[...] = (half[x_at].astype(f32) + x_in[...].astype(f32)).astype(bf16)
+        for hop in range(1, owners):
+            piece_copy(hop).start()
+
+    def sum_square():
+        value = piece[seq].astype(f32)
+        for hop in range(1, owners):
+            piece_copy(hop).wait()
+            value = value + piece_in[hop - 1].astype(f32)
+        part[...] = value.astype(bf16)
+        for hop in range(1, parts):
+            part_copy(hop).start()
+
+    def collect_square():
+        square_ref[batch] = part[...].astype(f32)
+        for hop in range(1, parts):
+            part_copy(hop).wait()
+            square_ref[lax.rem(batch + parts - hop, parts)] = part_in[hop - 1].astype(f32)
+
+    def seq_copies(hop):
+        target = lax.rem(seq + hop, owners)
+        return [
+            send(small_k.at[target], seq_k.at[hop - 1], sk_sem, hop - 1, "seq", target),
+            send(small_v, seq_v.at[hop - 1], sv_sem, hop - 1, "seq", target),
+        ]
+
+    def batch_copies(hop):
+        target = lax.rem(batch + hop, parts)
+        return [
+            send(mid_k, batch_k.at[hop - 1], bk_sem, hop - 1, "batch", target),
+            send(mid_v, batch_v.at[hop - 1], bv_sem, hop - 1, "batch", target),
+        ]
+
+    def reduce_small():
+        tall = small_k.shape[1]
+        keyval = gk_s[...].T
+        for o in range(owners):
+            small_k[o] = keyval[o * tall : (o + 1) * tall].astype(bf16)
+        small_v[...] = vec_s[...].astype(bf16)
+        for hop in range(1, owners):
+            for copy in seq_copies(hop):
+                copy.start()
+        value, vector = small_k[seq].astype(f32), small_v[...].astype(f32)
+        for hop in range(1, owners):
+            for copy in seq_copies(hop):
+                copy.wait()
+            value = value + seq_k[hop - 1].astype(f32)
+            vector = vector + seq_v[hop - 1].astype(f32)
+        mid_k[...] = value.astype(bf16)
+        mid_v[...] = vector.astype(bf16)
+        for hop in range(1, parts):
+            for copy in batch_copies(hop):
+                copy.start()
+        value, vector = mid_k[...].astype(f32), mid_v[...].astype(f32)
+        for hop in range(1, parts):
+            for copy in batch_copies(hop):
+                copy.wait()
+            value = value + batch_k[hop - 1].astype(f32)
+            vector = vector + batch_v[hop - 1].astype(f32)
+        keyval_ref[...] = value
+        vector_ref[...] = vector
+
+    def project():
+        branch, grad = bg_ref[...], gq_ref[0]
+        acc[0] += nn(att_ref[0], branch)
+        acc[1] += tt(normed_ref[...], grad)
+        ones = jnp.ones((8, branch.shape[0]), bf16)
+        vec_s[0:1] += nt(ones, grad)[0:1]
+        vec_s[1:2] += nn(ones, branch)[0:1]
+
+    def close(r):
+        act = jnp.concatenate([ref[...] for ref in acts], axis=1)
+        grad = jnp.concatenate([ref[...] for ref in ghs], axis=1)
+        branch = tn(att_ref[0], ow_ref[...]) + ob_ref[...]
+        branch = branch + (nn(act, down_ref[...]) + db_ref[...])
+        out_ref[...] = (x_ref[...].astype(f32) + valid_ref[...] * branch).astype(bf16)
+        gd_s[r] = nt(grad, up_ref[...])
+        gn_s[r] = tt(gq_ref[0], qw_ref[...])
+
+    def finish(r):
+        unit, spread = standardize(x_ref[...].astype(f32))
+        gain = ag_ref[...]
+        normed = (unit * gain + as_ref[...]).astype(bf16)
+        keyval = (total[r] + kcot_ref[0].astype(f32)).T
+        keyval = turn_back(keyval, cos_ref[...], sin_ref[...]).astype(bf16)
+        gk_s[...] += nn(keyval, normed)
+        vec_s[6:7, 0 : keyval.shape[0]] += nt(jnp.ones((8, keyval.shape[1]), bf16), keyval)[0:1]
+        first = gn_s[r] + tt(keyval, kw_ref[...])
+        second = gd_s[r]
+        vec_s[2:3] += jnp.sum(first * unit, axis=0, keepdims=True)
+        vec_s[3:4] += jnp.sum(first, axis=0, keepdims=True)
+        vec_s[4:5] += jnp.sum(second * unit, axis=0, keepdims=True)
+        vec_s[5:6] += jnp.sum(second, axis=0, keepdims=True)
+        both = first * gain + second * dg_ref[...]
+        middle = jnp.mean(both, axis=-1, keepdims=True)
+        along = jnp.mean(both * unit, axis=-1, keepdims=True)
+        gt_ref[...] = (cot_ref[...].astype(f32) + (both - middle - unit * along) * spread).astype(bf16)
+
+    def at(step):
+        return pl.when(i == step)
+
+    @at(0)
+    def _():
+        enter()
+        start_across(0)
+        acc[...] = jnp.zeros(acc.shape, f32)
+        gk_s[...] = jnp.zeros(gk_s.shape, f32)
+        vec_s[...] = jnp.zeros(vec_s.shape, f32)
+        for c in range(parts):
+            vec_s[8 + c : 9 + c] = gub_ref[c]
+
+    marks = (rows + 1, rows + 3, rows + 6, 2 * rows)
+    for step in range(planes):
+        @at(marks[step])
+        def _():
+            if step < planes - 1:
+                start_across(step + 1)
+            tick(step)
+
+    @at(rows)
+    def _():
+        cut_square()
+
+    @at(rows + 2)
+    def _():
+        halve_square()
+
+    @at(rows + 5)
+    def _():
+        spread_square()
+
+    @at(2 * rows + 2)
+    def _():
+        sum_square()
+
+    @at(2 * rows + 6)
+    def _():
+        collect_square()
+        settle()
+
+    @pl.when(i < rows)
+    def _():
+        project()
+
+    @pl.when((i >= rows) & (i < 2 * rows))
+    def _():
+        close(i - rows)
+
+    @pl.when((i >= 2 * rows) & (i < 3 * rows))
+    def _():
+        finish(i - 2 * rows)
+
+    @at(3 * rows)
+    def _():
+        reduce_small()
+
+
+def tail(
+    x, cot, valid, att, gq, bg, normed, kcot, terms, gub, ow, ob, down, db, up, qw, kw, again, ashift,
+    dgain, cos, sin, act, gh, parts, owners, dense_tile=512,
+):
+    rows, width, blk = att.shape
+    tok, ff, kvw = rows * blk, up.shape[1], kw.shape[1]
+    ratio, tiles = dense_tile // blk, tok // dense_tile
+    planes = owners // 2
+    high, cols, tall = width // owners // 2, width // 2, width // owners
+    once = lambda *shape: pl.BlockSpec(
+        shape, lambda i: (0,) * len(shape), pipeline_mode=pl.Buffered(1)
+    )
+    one = lambda i: jnp.clip(i, 0, rows - 1)
+    two = lambda i: jnp.where(i < 2 * rows, i % rows, rows - 1)
+    middle = lambda i: jnp.clip(i - rows, 0, rows - 1)
+    late = lambda i: jnp.clip(i - 2 * rows, 0, rows - 1)
+    both = lambda i: jnp.where(i < 2 * rows, middle(i), late(i))
+    flat = lambda of, w=width: pl.BlockSpec((blk, w), lambda i: (of(i), 0))
+    stack = lambda of, h, w: pl.BlockSpec((1, h, w), lambda i: (of(i), 0, 0))
+    wide = [
+        pl.BlockSpec(
+            (blk, ff // parts),
+            lambda i, c=c: ((c * tiles + middle(i) // ratio + 1) * ratio + middle(i) % ratio, 0),
+        )
+        for c in range(parts)
+    ]
+    dma = pltpu.SemaphoreType.DMA
+    vmem = lambda kind, *shape: pltpu.VMEM(shape, kind)
+    return pl.pallas_call(
+        partial(tail_kernel, rows=rows, parts=parts, owners=owners),
+        grid=(3 * rows + 1,),
+        in_specs=[
+            flat(both), flat(late), flat(middle, 1), stack(two, width, blk), stack(two, width, blk),
+            flat(one), flat(one), stack(late, blk, kvw), pl.BlockSpec(memory_space=pl.ANY),
+            once(parts, 1, ff // parts),
+            once(width, width), once(1, width), once(ff, width), once(1, width), once(width, ff),
+            once(width, width), once(width, kvw), once(1, width), once(1, width), once(1, width),
+            once(ROT_HALF, blk), once(ROT_HALF, blk),
+        ] + wide + wide,
+        out_specs=[
+            flat(middle), flat(late), once(parts, 2, high, cols), once(tall, kvw), once(16, width),
+        ],
+        out_shape=[
+            jax.ShapeDtypeStruct((tok, width), bf16),
+            jax.ShapeDtypeStruct((tok, width), bf16),
+            jax.ShapeDtypeStruct((parts, 2, high, cols), f32),
+            jax.ShapeDtypeStruct((tall, kvw), f32),
+            jax.ShapeDtypeStruct((16, width), f32),
+        ],
+        scratch_shapes=[
+            vmem(f32, 2, width, width), vmem(f32, rows, blk, width), vmem(f32, rows, blk, width),
+            vmem(f32, kvw, width), vmem(f32, 16, width),
+            vmem(bf16, planes, rows, blk, kvw), vmem(bf16, planes, rows, blk, kvw),
+            vmem(bf16, planes, rows, blk, kvw), vmem(f32, rows, blk, kvw),
+            vmem(bf16, 2, 2, owners, 2, high, cols), vmem(bf16, 2, owners, 2, high, cols),
+            vmem(bf16, 2, owners, 2, high, cols), vmem(bf16, owners, 2, high, cols),
+            vmem(bf16, owners, 2, high, cols), vmem(bf16, owners - 1, 2, high, cols),
+            vmem(bf16, 2, high, cols), vmem(bf16, parts - 1, 2, high, cols),
+            vmem(bf16, owners, tall, kvw), vmem(bf16, 16, width),
+            vmem(bf16, owners - 1, tall, kvw), vmem(bf16, owners - 1, 16, width),
+            vmem(bf16, tall, kvw), vmem(bf16, 16, width),
+            vmem(bf16, parts - 1, tall, kvw), vmem(bf16, parts - 1, 16, width),
+            dma((planes,)), dma((2, planes)), dma((2, planes)), dma((2, 1)), dma((2, 1)),
+            dma((2, owners - 1)), dma((2, parts - 1)), dma((2, owners - 1)), dma((2, owners - 1)),
+            dma((2, parts - 1)), dma((2, parts - 1)),
+        ],
+        compiler_params=params(62, collective_id=1, has_side_effects=True),
+        cost_estimate=cost(4 * tok * width * (2 * width + ff), 4 * tok * ff + 20 * tok * width),
+        name="tail",
+    )(
+        x, cot, valid, att, gq, bg, normed, kcot, terms, gub, ow, ob, down, db, up, qw, kw, again,
+        ashift, dgain, cos, sin, *[act] * parts, *[gh] * parts,
+    )
+
+
+def attn_kernel(first_ref, sidx_ref, q_ref, do_ref, kv_ref, start_ref, cos_ref, sin_ref,
+                att_ref, gq_ref, dkv_ref,
+                qz, dz, p_s, m_s, bias_s, o_s, mx, ls, dq_s, dc_s, inn_s, ds_s, ic_s, *, blk, nblk):
+    r = pl.program_id(0)
+    L = HEADS*blk
+    e = sidx_ref[0]
+    n = e - first_ref[r] + 1
+    qz[0:HEAD_DIM,:] = q_ref[0]
+    qz[HEAD_DIM:,:] = jnp.zeros((HEAD_DIM,L),bf16)
+    dz[0:HEAD_DIM,:] = jnp.zeros((HEAD_DIM,L),bf16)
+    mx[...] = jnp.full((1,L),negative,f32)
+    ls[...] = jnp.zeros((1,L),f32)
+    o_s[...] = jnp.zeros((HEAD_DIM,L),f32)
+    dq_s[...] = jnp.zeros((HEAD_DIM,L),f32)
+    start = start_ref[0]
+    qpos = e*blk + lax.broadcasted_iota(jnp.int32,(1,blk),1)
+    krow = lax.broadcasted_iota(jnp.int32,(blk,blk),0)
+
+    @pl.loop(0, nblk)
+    def _(j):
+        @pl.when((j < first_ref[r]) | (j > e))
+        def _():
+            dkv_ref[j,0] = jnp.zeros((blk,2*HEAD_DIM),bf16)
+
+    @pl.loop(0, n)
+    def _(jj):
+        j = e - jj
+        kvj = kv_ref[j, 0, 0:blk, :]
+        vt = kvj.T[HEAD_DIM:,:]
+        kpos = j*blk + krow
+        bias_s[...] = jnp.where((kpos>=start)&(kpos<=qpos), 0.0, negative)
+        def hsl(h): return slice(h*blk,(h+1)*blk)
+        sv = {}; pv = {}; av = {}
+        for h in range(HEADS+2):
+            if h < HEADS:
+                sv[h] = nn(kvj, qz[:,hsl(h)])
+            if 0 <= h-2 < HEADS:
+                g = h-2; hs = hsl(g)
+                o_s[:,hs] = o_s[:,hs]*av.pop(g) + nn(vt,pv.pop(g))
+            if 0 <= h-1 < HEADS:
+                g = h-1; hs = hsl(g)
+                s = sv.pop(g)*LOG2E + bias_s[...]
+                mo = mx[:,hs]
+                mn = jnp.maximum(mo, jnp.max(s,axis=0,keepdims=True))
+                p = jnp.exp2(s-mn)
+                a = jnp.exp2(mo-mn)
+                ls[:,hs] = ls[:,hs]*a + jnp.sum(p,axis=0,keepdims=True)
+                pb = p.astype(bf16)
+                p_s[jj,:,hs] = pb
+                m_s[jj,:,hs] = mn
+                mx[:,hs] = mn
+                pv[g]=pb; av[g]=a
+
+    inv = 1.0/ls[...]
+    o = o_s[...]*inv
+    for h in range(HEADS):
+        att_ref[0, h*HEAD_DIM:(h+1)*HEAD_DIM, :] = o[:, h*blk:(h+1)*blk].astype(bf16)
+    do = do_ref[0].astype(f32)
+    inn_s[...] = jnp.sum(o*do,axis=0,keepdims=True)
+    ls[...] = inv
+
+    @pl.loop(0, n)
+    def _(jj):
+        j = e - jj
+        kvj = kv_ref[j, 0, 0:blk, :]
+        kt = kvj.T[:HEAD_DIM,:]
+        def hsl(h): return slice(h*blk,(h+1)*blk)
+        c = jnp.exp2(m_s[jj]-mx[...])*ls[...]
+        dc_s[...] = (do_ref[0].astype(f32)*c).astype(bf16)
+        dz[HEAD_DIM:,:] = dc_s[...]
+        ic_s[...] = inn_s[...]*c
+        dpv = {}; dsv = {}
+        for h in range(HEADS+2):
+            if h < HEADS:
+                dpv[h] = nn(kvj, dz[:,hsl(h)])
+            if 0 <= h-2 < HEADS:
+                g = h-2; hs = hsl(g)
+                dq_s[:,hs] = dq_s[:,hs] + nn(kt, dsv.pop(g))
+            if 0 <= h-1 < HEADS:
+                g = h-1; hs = hsl(g)
+                pb = p_s[jj,:,hs]
+                ds = (pb.astype(f32)*(dpv.pop(g)-ic_s[:,hs])).astype(bf16)
+                ds_s[:,hs] = ds
+                dsv[g] = ds
+        dv = nt(p_s[jj], dc_s[...])
+        dk = nt(ds_s[...], qz[0:HEAD_DIM,:])
+        dkv_ref[j,0] = jnp.concatenate([dk,dv],axis=1).astype(bf16)
+
+    cos = cos_ref[...]; sin = sin_ref[...]
+    for h in range(HEADS):
+        g = dq_s[:, h*blk:(h+1)*blk]*(HEAD_DIM**-0.5)
+        a, b = g[0:8], g[8:16]
+        gq_ref[0, h*HEAD_DIM:(h+1)*HEAD_DIM, :] = jnp.concatenate([a*cos+b*sin, b*cos-a*sin, g[16:]],axis=0).astype(bf16)
+
+def attention(first, sidx, qT, doT, kv, start, cosT, sinT):
+    rows, _, L = qT.shape
+    blk = L//HEADS
+    nblk = kv.shape[0]
+    gs = pltpu.PrefetchScalarGridSpec(
+        num_scalar_prefetch=2, grid=(rows,),
+        in_specs=[
+            pl.BlockSpec((1,HEAD_DIM,L),lambda r,*_:(r,0,0)),
+            pl.BlockSpec((1,HEAD_DIM,L),lambda r,*_:(r,0,0)),
+            pl.BlockSpec((nblk,1,blk+16,2*HEAD_DIM),lambda r,*_:(0,r,0,0)),
+            pl.BlockSpec((1,1,blk),lambda r,*_:(r,0,0)),
+            pl.BlockSpec((8,blk),lambda r,*_:(0,0)),
+            pl.BlockSpec((8,blk),lambda r,*_:(0,0)),
+        ],
+        out_specs=[
+            pl.BlockSpec((1,HEADS*HEAD_DIM,blk),lambda r,*_:(r,0,0)),
+            pl.BlockSpec((1,HEADS*HEAD_DIM,blk),lambda r,*_:(r,0,0)),
+            pl.BlockSpec((nblk,1,blk,2*HEAD_DIM),lambda r,*_:(0,r,0,0)),
+        ],
+        scratch_shapes=[
+            pltpu.VMEM((2*HEAD_DIM,L),bf16), pltpu.VMEM((2*HEAD_DIM,L),bf16),
+            pltpu.VMEM((nblk,blk,L),bf16), pltpu.VMEM((nblk,1,L),f32),
+            pltpu.VMEM((blk,blk),f32), pltpu.VMEM((HEAD_DIM,L),f32),
+            pltpu.VMEM((1,L),f32), pltpu.VMEM((1,L),f32),
+            pltpu.VMEM((HEAD_DIM,L),f32), pltpu.VMEM((HEAD_DIM,L),bf16), pltpu.VMEM((1,L),f32), pltpu.VMEM((blk,L),bf16), pltpu.VMEM((1,L),f32),
+        ])
+    return pl.pallas_call(
+        partial(attn_kernel, blk=blk, nblk=nblk),
+        out_shape=[jax.ShapeDtypeStruct((rows,HEADS*HEAD_DIM,blk),bf16),
+                   jax.ShapeDtypeStruct((rows,HEADS*HEAD_DIM,blk),bf16),
+                   jax.ShapeDtypeStruct((nblk,rows,blk,2*HEAD_DIM),bf16)],
+        grid_spec=gs,
+        compiler_params=params(56),
+        cost_estimate=cost(6e10, 4e7),
+        name="attention",
+    )(first, sidx, qT, doT, kv, start, cosT, sinT)
+
+
+def local(
+    tokens,
+    segment_ids,
+    query_weight,
+    query_bias,
+    keyval_weight,
+    keyval_bias,
+    out_weight,
+    out_bias,
+    up_weight,
+    up_bias,
+    down_weight,
+    down_bias,
+    attention_gain,
+    attention_shift,
+    dense_gain,
+    dense_shift,
+    out_cotangent,
+    keyval_cotangent,
+):
+    rows, blk, width = tokens.shape
+    ff = up_weight.shape[1]
+    kvw = 2 * HEAD_DIM
+    tok = rows * blk
+    owners, parts = lax.axis_size("seq"), lax.axis_size("batch")
+    place = lax.axis_index("seq")
+    cos, sin = rotary_tables(place * blk + jnp.arange(blk, dtype=jnp.int32))
+    cos, sin = cos.T, sin.T
+    live = jnp.sum((segment_ids >= 0).astype(jnp.int32), axis=1).astype(jnp.int32)
+    x = tokens.reshape(tok, width)
+    cot = out_cotangent.reshape(tok, width)
+    row = lambda vector: vector.reshape(1, -1)
+
+    normed, dense_in, keyval, branch_grad = norms(
+        live, x, cot, segment_ids.reshape(rows, blk // 128, 128), row(attention_gain),
+        row(attention_shift), row(dense_gain), row(dense_shift), keyval_weight, row(keyval_bias),
+        cos, sin, rows, blk,
+    )
+    act, grad_hidden, mlp, gub, keyval_all = dense(
+        dense_in, branch_grad, up_weight, row(up_bias), down_weight, keyval, parts, owners
+    )
+    queries, grad_attended = heads(
+        normed, branch_grad, query_weight, row(query_bias), out_weight, cos, sin, rows, blk
+    )
+    mlp = lax.psum_scatter(mlp, "seq", scatter_dimension=0)
+    mlp = lax.all_gather(mlp, "batch").astype(f32)
+    high, half = width // owners // 2, ff // parts // 2
+    grad_up_weight = (
+        mlp[:, : parts * high]
+        .reshape(2, 2, parts, high, half)
+        .transpose(1, 3, 2, 0, 4)
+        .reshape(width // owners, ff)
+    )
+    grad_down_weight = (
+        mlp[:, parts * high :]
+        .reshape(2, 2, ff // owners // 2, half)
+        .transpose(1, 2, 0, 3)
+        .reshape(ff // owners, width)
+    )
+
+    ids = keyval_all[:, :, blk : blk + blk // 128, :].reshape(owners, rows, blk).astype(f32)
+    before = (jnp.arange(owners) <= place)[:, None, None]
+    order = lambda values: jnp.where(values < 0, 1024.0, values)
+    ids = jnp.where(before, order(ids), 2048.0)
+    start = jnp.sum(
+        (ids[:, :, None, :] < order(segment_ids.astype(f32))[None, :, :, None]).astype(jnp.int32),
+        axis=(0, 3),
+    ).astype(jnp.int32)
+    attended, grad_query, terms = attention(
+        start[:, 0] // blk, place.astype(jnp.int32)[None], queries, grad_attended, keyval_all,
+        start[:, None, :], cos, sin,
+    )
+    valid = (segment_ids >= 0).astype(f32).reshape(tok, 1)
+    layer_out, grad_tokens, square, grad_keyval_weight, vectors = tail(
+        x, cot, valid, attended, grad_query, branch_grad, normed, keyval_cotangent, terms, gub,
+        out_weight, row(out_bias), down_weight, row(down_bias), up_weight, query_weight,
+        keyval_weight, row(attention_gain), row(attention_shift), row(dense_gain), cos, sin, act,
+        grad_hidden, parts, owners,
+    )
+    square = (
+        square.reshape(2, 2, 2, high, width // 2)
+        .transpose(2, 1, 3, 0, 4)
+        .reshape(2, width // owners, width)
+    )
+    share = width // owners
+    mine = lambda vector, size: lax.dynamic_slice(vector, (place * size,), (size,))
+    query_bias_grad, branch_sum, ag, ash, dg, dsh = [mine(vectors[i], share) for i in range(6)]
+    return (
+        layer_out.reshape(rows, blk, width),
+        keyval[:, :blk, :],
+        grad_tokens.reshape(rows, blk, width),
+        square[1],
+        query_bias_grad,
+        grad_keyval_weight,
+        mine(vectors[6], kvw // owners),
+        square[0],
+        branch_sum,
+        grad_up_weight,
+        mine(vectors[8 : 8 + parts].reshape(ff), ff // owners),
+        grad_down_weight,
+        branch_sum,
+        ag,
+        ash,
+        dg,
+        dsh,
+    )
+
+
+def choose(tokens, *rest):
+    fits = tokens.shape[1] % 128 == 0 and lax.axis_size("batch") == 4 and lax.axis_size("seq") == 8
+    return (local if fits else local_plain)(tokens, *rest)
+
+
 def solution(mesh):
     placed = (
         P("batch", "seq", None),
@@ -349,7 +1353,7 @@
         P("batch", "seq", None),
     )
     return jax.shard_map(
-        local,
+        choose,
         mesh=mesh,
         in_specs=placed,
         out_specs=(

time: 1880 us -> 381 us (0.20)
  matrix products: 860 us -> 0 us
  local copies, waits for them, and re-layouts: 411 us -> 43.7 us
  Pallas kernels: 0 us -> 309 us
  other arithmetic: 298 us -> 4.3 us
  waiting for transfers between devices: 199 us -> 11 us
  blocking collectives: 81.4 us -> 0 us
    dot_general x71 -> x0, matrix products: 860 us -> none  [the longest x29 411 us: contract_cols(): lax.dot_general(left_side, right_side, (((1,), (1,)), ((), ())), preferre...]
    pallas_call x0 -> x5, Pallas kernels: none -> 309 us  [the longest x1 166 us: tail(): pl.pallas_call(partial(tail_kernel, rows=rows, parts=parts, owners=owners...]
    broadcast_in_dim x32 -> x1, local copies, waits for them, and re-layouts: 230 us -> 0.61 us  [local(): start[:, None, :]]
    reduce_scatter x6 -> x1, waiting for transfers between devices: 198 us -> 11 us  [local(): mlp = lax.psum_scatter(mlp, 'seq', scatter_dimension=0)]
    convert_element_type x26 -> x1, other arithmetic: 164 us -> 0.92 us  [local(): keyval_all[:, :, blk:blk + blk // 128, :].reshape(owners, rows, blk)]
    reduce_sum x14 -> x2, other arithmetic: 114 us -> 2.63 us  [the longest x1 1.82 us: local(): jnp.sum((ids[:, :, None, :] < order(segment_ids.astype(f32))[None, :, :,...]
    while x32 -> x0, local copies, waits for them, and re-layouts: 36.2 us -> none
    unnamed x1 -> x0, blocking collectives: 35.9 us -> none
  transfers between devices with their start and end apart: 8 -> 2, of which waited for: 4 -> 1; matrix products, arithmetic and copies ran while one was open for 80% -> 4% of each run, Pallas kernels for 0% -> 55%
where the time goes in v2:
time: 381 us; the launch traced here: 382 us
  Pallas kernels  309 us (81%)
  local copies, waits for them, and re-layouts  43.7 us (11%)
  between operations  14.3 us (4%)
  waiting for transfers between devices  11 us (3%)
  other arithmetic  4.3 us (1%)
    pallas_call x1, Pallas kernels, tail(): pl.pallas_call(partial(tail_kernel, rows=rows, parts=parts, owners=owners...  166 us
    pallas_call x1, Pallas kernels, dense(): pl.pallas_call(partial(dense_kernel, pairs=pairs, steps=steps, tile=tile,...  92.1 us
    pallas_call x1, Pallas kernels, attention(): pl.pallas_call(partial(attn_kernel, blk=blk, nblk=nblk), out_shape=[jax.S...  36 us
    unnamed x59, local copies, waits for them, and re-layouts  26 us
    reduce_scatter x1, waiting for transfers between devices, local(): mlp = lax.psum_scatter(mlp, 'seq', scatter_dimension=0)  11 us
    pallas_call x1, Pallas kernels, heads(): pl.pallas_call(heads_kernel, grid=(rows,), in_specs=[tile, tile, whole(wi...  8.04 us
  transfers between devices with their start and end apart: 2, of which 1 were waited for; matrix products, arithmetic and copies ran while one was open for 4% of the time, Pallas kernels for 55%

profile of v2, /device:TPU:0, one launch (start us, length us, event | category | flops | bytes accessed | tf_op | source)
XLA Modules:
  0.0 382.2 jit_solution(3020430269869511028)
XLA Ops:
  7.3 0.8 convert_reduce_fusion.1
  11.7 1.9 copy-done
  13.6 1.9 copy-done.1
  15.5 0.9 copy-done.6
  17.1 6.8 %norms.1 = (bf16[2048,768]{1,0:T(8,128)(2,1)S(1)}, bf16[2048,768]{1,0:T(8,128)(2,1)S(1)}, bf16[8,272,128]{2,1,0:T(8,128)(2,1)S(1)}, bf16[2048,768]{1,0:T(8,128)(2,1)S(1)}) custom-call(s32[8]{0:T(128)S(1)} %get-tuple-element.55.live_ref, bf16[2048,768]{1,0:T(8,128)(2,1)S(1)} %bitcast.45, bf16[2048,768]{1,0:T(8,128)(2,1)S(1)} %bitcast.47, ...), custom_call_target="tpu_custom_call" | custom-call | flops 402653184 | bytes 15728640 | tf_op jit(solution)/shard_map/norms/pallas_call | solution.py:407
  23.9 1.7 copy-done.3
  25.6 0.8 copy-done.7
  26.4 1.7 copy-done.15
  28.1 92.1 %dense.1 = (bf16[9216,768]{1,0:T(8,128)(2,1)}, bf16[9216,768]{1,0:T(8,128)(2,1)}, bf16[8,384,384]{2,1,0:T(8,128)(2,1)}, f32[4,1,768]{2,1,0:T(1,128)}, bf16[8,8,272,128]{3,2,1,0:T(8,128)(2,1)}) custom-call(bf16[2048,768]{1,0:T(8,128)(2,1)} %copy-done.15, bf16[2048,768]{1,0:T(8,128)(2,1)} %copy-done.3, bf16[768,3072]{1,0:T(8,128)(2,1)} %up_ref.3, ...), custom_call_target="tpu_custom_call" | custom-call | flops 38654705664 | bytes 37748736 | tf_op jit(solution)/shard_map/dense/pallas_call | solution.py:704
  120.3 0.9 slice_convert_fusion
  121.3 1.8 convert_reduce_fusion
  125.1 1.3 copy.55
  127.0 1.3 copy-done.4
  128.2 1.3 copy-done.5
  129.5 8.0 %heads.1 = (bf16[8,64,3072]{2,1,0:T(8,128)(2,1)S(1)}, bf16[8,64,3072]{2,1,0:T(8,128)(2,1)S(1)}) custom-call(bf16[2048,768]{1,0:T(8,128)(2,1)S(1)} %get-tuple-element.40.normed_ref, bf16[2048,768]{1,0:T(8,128)(2,1)} %copy-done.3, bf16[768,768]{1,0:T(8,128)(2,1)S(1)} %copy-done.4, f32[1,768]{1,0:T(1,128)S(1)} %reshape.153.qb_ref, ...), custom_call_target="tpu_custom_call" | custom-call | flops 4831838208 | bytes 12582912 | tf_op jit(solution)/shard_map/heads/pallas_call | solution.py:454
  137.6 1.7 copy-done.16
  139.2 1.6 copy-done.17
  140.9 36.0 %attention.1 = (bf16[8,768,256]{2,1,0:T(8,128)(2,1)}, bf16[8,768,256]{2,1,0:T(8,128)(2,1)}, bf16[8,8,256,128]{3,2,1,0:T(8,128)(2,1)}) custom-call(s32[8]{0:T(128)} %and_select_fusion.first_ref, s32[1]{0:T(128)} %bitcast.4.sidx_ref, bf16[8,64,3072]{2,1,0:T(8,128)(2,1)} %copy-done.16, bf16[8,64,3072]{2,1,0:T(8,128)(2,1)} %copy-done.17, ...), custom_call_target="tpu_custom_call" | custom-call | flops 60000002048 | bytes 40000000 | tf_op jit(solution)/shard_map/attention/pallas_call | solution.py:1209
  176.8 11.0 %reduce-scatter.2.cloned.1.call-done = bf16[1,384,384]{2,1,0:T(8,128)(2,1)} async-done(((bf16[8,384,384]{2,1,0:T(8,128)(2,1)}), bf16[1,384,384]{2,1,0:T(8,128)(2,1)}) %reduce-scatter.2.cloned.1.call-update) | async-done | bytes 294928 | tf_op jit(solution)/shard_map/reduce_scatter | solution.py:1265
  187.9 165.9 %tail.1 = (bf16[2048,768]{1,0:T(8,128)(2,1)}, bf16[2048,768]{1,0:T(8,128)(2,1)}, f32[4,2,48,384]{3,2,1,0:T(8,128)}, f32[96,128]{1,0:T(8,128)}, f32[16,768]{1,0:T(8,128)}) custom-call(bf16[2048,768]{1,0:T(8,128)(2,1)} %bitcast.44, bf16[2048,768]{1,0:T(8,128)(2,1)} %bitcast.46, f32[2048,1]{1,0:T(8,128)} %bitcast.52, ...), custom_call_target="tpu_custom_call" | custom-call | flops 28991029248 | bytes 56623104 | tf_op jit(solution)/shard_map/tail/pallas_call | solution.py:1042
  353.8 0.8 slice.49
  354.6 0.7 slice.56
  355.4 1.0 fusion.10
  357.0 1.1 fusion.9
  358.3 0.7 copy.57
  362.4 1.4 fusion.8
  363.8 0.9 copy.53
  364.7 1.1 copy.58
  365.8 0.9 copy.52
  366.7 2.0 reshape.160
  369.2 3.9 %copy.64 = bf16[8,256,768]{2,1,0:T(8,128)(2,1)} copy(bf16[8,256,768]{2,1,0:T(8,128)(2,1)} %bitcast.54) | data formatting | bytes 6291456
  373.1 1.7 copy.65
  (76 shorter events, 12.4 us)
Async XLA Ops:
  7.2 180.6 %reduce-scatter.2.cloned.1.call-start = ((), (), s32[]{:S(2)}) async-start(), calls=%async_computation.1 | async-start | bytes 2654208 | tf_op jit(solution)/shard_map/reduce_scatter | solution.py:1265
  9.5 14.4 %copy-start.11 = (f32[1,768]{1,0:T(1,128)}, f32[1,768]{1,0:T(1,128)S(1)}, u32[]{:S(2)}) copy-start(f32[1,768]{1,0:T(1,128)S(1)} %reshape.147.ag_ref) | copy-start | bytes 9220
  10.2 13.7 %copy-start.12 = (f32[1,768]{1,0:T(1,128)}, f32[1,768]{1,0:T(1,128)S(1)}, u32[]{:S(2)}) copy-start(f32[1,768]{1,0:T(1,128)S(1)} %reshape.148.as_ref) | copy-start | bytes 9220
  10.9 13.0 %copy-start.13 = (f32[1,768]{1,0:T(1,128)}, f32[1,768]{1,0:T(1,128)S(1)}, u32[]{:S(2)}) copy-start(f32[1,768]{1,0:T(1,128)S(1)} %reshape.149.dg_ref) | copy-start | bytes 9220
  11.7 115.3 %copy-start.9 = (f32[8,256]{1,0:T(8,128)}, f32[8,256]{1,0:T(8,128)S(1)}, u32[]{:S(2)}) copy-start(f32[8,256]{1,0:T(8,128)S(1)} %get-tuple-element.68.sin_ref) | copy-start | bytes 24580
  11.7 115.3 %copy-start.10 = (f32[8,256]{1,0:T(8,128)}, f32[8,256]{1,0:T(8,128)S(1)}, u32[]{:S(2)}) copy-start(f32[8,256]{1,0:T(8,128)S(1)} %get-tuple-element.69.cos_ref) | copy-start | bytes 24580
  11.7 1.9 copy-start
  13.6 1.9 copy-start.1
  15.5 0.9 copy-start.6
  16.4 0.7 copy-start.14
  23.9 1.7 copy-start.3
  25.6 0.8 copy-start.7
  26.4 1.7 copy-start.15
  28.1 98.9 %copy-start.2 = (bf16[2048,768]{1,0:T(8,128)(2,1)}, bf16[2048,768]{1,0:T(8,128)(2,1)S(1)}, u32[]{:S(2)}) copy-start(bf16[2048,768]{1,0:T(8,128)(2,1)S(1)} %get-tuple-element.40.normed_ref) | copy-start | bytes 9437188
  28.1 92.2 %copy-start.19 = (s32[8,256]{1,0:T(8,128)S(1)}, s32[8,256]{1,0:T(8,128)}, u32[]{:S(2)}) copy-start(s32[8,256]{1,0:T(8,128)} %param.19) | copy-start | bytes 24580
  28.1 95.8 %copy-start.21 = (f32[768]{0:T(1024)S(1)}, f32[768]{0:T(1024)}, u32[]{:S(2)}) copy-start(f32[768]{0:T(1024)} %param.21) | copy-start | bytes 9220
  28.1 95.8 %copy-start.22 = (f32[768]{0:T(1024)S(1)}, f32[768]{0:T(1024)}, u32[]{:S(2)}) copy-start(f32[768]{0:T(1024)} %param.25) | copy-start | bytes 9220
  28.1 96.4 %copy-start.23 = (f32[768]{0:T(1024)S(1)}, f32[768]{0:T(1024)}, u32[]{:S(2)}) copy-start(f32[768]{0:T(1024)} %param.29) | copy-start | bytes 9220
  120.2 242.2 %all-gather.2.cloned.1.call-start = ((), (), s32[]{:S(2)}) async-start(), calls=%async_computation.2 | async-start | bytes 1474560 | tf_op jit(solution)/shard_map/all_gather | solution.py:1266
  127.0 1.3 copy-start.4
  128.2 1.3 copy-start.5
  137.5 1.7 copy-start.16
  139.2 1.6 copy-start.17
  187.8 165.9 %copy-start.8 = (bf16[8,272,128]{2,1,0:T(8,128)(2,1)S(1)}, bf16[8,272,128]{2,1,0:T(8,128)(2,1)}, u32[]{:S(2)}) copy-start(bf16[8,272,128]{2,1,0:T(8,128)(2,1)} %copy-done.7) | copy-start | bytes 1671172
  357.0 11.7 %copy-start.24 = (f32[96]{0:T(128)}, f32[96]{0:T(128)S(1)}, u32[]{:S(2)}) copy-start(f32[96]{0:T(128)S(1)} %get-tuple-element.135) | copy-start | bytes 1156
  369.2 3.9 %copy-start.18 = (bf16[2048,768]{1,0:T(8,128)(2,1)S(1)}, bf16[2048,768]{1,0:T(8,128)(2,1)}, u32[]{:S(2)}) copy-start(bf16[2048,768]{1,0:T(8,128)(2,1)} %get-tuple-element.50) | copy-start | bytes 9437188
  373.1 1.7 copy-start.20
Sparse Core Ops, SparseCore 0:
  120.3 67.4 reduce-scatter.1
  189.4 89.1 all-gather.1
